TPU v7x, 512 devices: a whole 4x8x8 slice. The times are simulated.
512 devices in a mesh: tm: 128 (over z_hi, x, y), rows: 4 (over z_lo, core).
Axes of the slice: x: 4, y: 8, z: 8 (z_hi: 4, z_lo: 2; z = z_hi * 2 + z_lo), core: 2. Of those that a mesh axis runs over, the one named last changes fastest.
Arguments:
- stream: bfloat16 [512, 32, 96, 128], P('tm', 'rows'), may hold values from -6 to 6
- gains: float32 [2, 96], replicated, may hold values from 0.5 to 2
- kernels: bfloat16 [2, 3, 3, 3, 96, 96], replicated, may hold values from -0.125 to 0.125
- biases: float32 [2, 96], replicated, may hold values from -3 to 3
Outputs:
- decoded: bfloat16 [512, 32, 96, 128], P('tm', 'rows')
All inputs are finite; a program needn't handle non-finite values.
Results may differ from a plain program's by a relative error of at most 0.0039.
Values may be sent and summed in bfloat16 or wider, within the bound.
No kernel may reach another device: no remote copies, remote signals or barrier semaphores. Data moves between devices by JAX's collectives and lax.ppermute only.
A program may use at most 64 MiB of HBM per device.

v0:
```python
import jax
import jax.numpy as jnp
from jax import lax
from jax.sharding import PartitionSpec as P

EPS = 1e-06


def with_halo(x, sides, width):
    for axis, dim in sides:
        size, length = (lax.axis_size(axis), x.shape[dim])
        up = [(i, (i + 1) % size) for i in range(size - 1)]
        down = [(j, i) for i, j in up]
        last = lax.slice_in_dim(x, length - width, length, axis=dim)
        first = lax.slice_in_dim(x, 0, width, axis=dim)
        before = lax.ppermute(last, axis, up)
        after = lax.ppermute(first, axis, down)
        x = jnp.concatenate([before, x, after], axis=dim)
    return x


def shifted(block, axis, distance):
    devices = range(lax.axis_size(axis))
    route = [(i - distance, i) for i in devices if i - distance in devices]
    return lax.ppermute(block, axis, route)


def channel_norm(values, gain):
    floats = values.astype(jnp.float32)
    mean_sq = jnp.mean(floats * floats, axis=2, keepdims=True)
    scaled = floats * lax.rsqrt(mean_sq + EPS) * gain[None, None, :, None]
    return jax.nn.silu(scaled).astype(jnp.bfloat16)


def valid_conv(extended, kernel, bias):
    banded = with_halo(extended, (("rows", 1),), 1)
    padded = jnp.pad(banded, ((0, 0), (0, 0), (0, 0), (1, 1)))
    out_len = extended.shape[0] - 2
    row_count = extended.shape[1]
    channels = extended.shape[2]
    col_count = extended.shape[3]
    summed = jnp.zeros((out_len, row_count, kernel.shape[4], col_count), jnp.float32)
    for tap_t in range(3):
        stacked = jnp.concatenate(
            [
                padded[
                    tap_t : tap_t + out_len, tap_r : tap_r + row_count, :, tap_w : tap_w + col_count
                ]
                for tap_r in range(3)
                for tap_w in range(3)
            ],
            axis=2,
        )
        summed = summed + jnp.einsum(
            "trkw,ko->trow",
            stacked,
            kernel[tap_t].reshape(9 * channels, -1),
            preferred_element_type=jnp.float32,
        )
    return summed + bias[None, None, :, None]


def with_history(normed):
    earlier = shifted(normed[-2:], "tm", 1)
    return jnp.concatenate([earlier, normed], axis=0)


def shards(stream, gains, kernels, biases):
    current = stream
    hidden = valid_conv(with_history(channel_norm(current, gains[0])), kernels[0], biases[0])
    branch = valid_conv(with_history(channel_norm(hidden, gains[1])), kernels[1], biases[1])
    current = (current.astype(jnp.float32) + branch).astype(jnp.bfloat16)
    return current


def solution(mesh):
    placed = (P("tm", "rows", None, None), P(), P(), P())
    return jax.shard_map(
        shards, mesh=mesh, in_specs=placed, out_specs=P("tm", "rows", None, None), check_vma=False
    )
```

profile of v0, /device:TPU:257, one launch (start us, length us, event | category | flops | bytes accessed | tf_op | source)
XLA Modules:
  0.0 101.3 jit_solution(16364331994366439794)
XLA Ops:
  0.0 0.8 slice_bitcast_fusion.1
  0.8 1.3 %fusion.11 = f32[4,8,128]{2,1,0:T(8,128)S(1)} fusion(bf16[4,8,96,128]{3,2,1,0:T(8,128)(2,1)} %param.4), kind=kLoop, calls=%fused_computation.18 | loop fusion | flops 1175552 | bytes 802816 | tf_op jit(solution)/shard_map/reduce_sum | solution.py:30
  2.1 1.7 %fusion.18 = bf16[4,8,96,128]{3,2,1,0:T(8,128)(2,1)S(1)} fusion(bf16[4,8,96,128]{3,2,1,0:T(8,128)(2,1)} %param.4, f32[96]{0:T(128)S(1)} %get-tuple-element.76, f32[4,8,128]{2,1,0:T(8,128)S(1)} %add_rsqrt_fusion.1), kind=kLoop, calls=%fused_computation.25 | loop fusion | flops 3145728 | bytes 1589632 | tf_op jit(solution)/shard_map/convert_element_type | solution.py:32
  3.8 3.2 %collective-permute-start = (bf16[2,8,96,128]{3,2,1,0:T(8,128)(2,1)S(1)}, bf16[2,8,96,128]{3,2,1,0:T(8,128)(2,1)S(1)}, u32[]{:S(2)}, u32[]{:S(2)}) collective-permute-start(bf16[2,8,96,128]{3,2,1,0:T(8,128)(2,1)S(1)} %slice.324), channel_id=1, source_target_pairs={{0,4},{4,8},{8,12},{12,16},{16,20},{20,24},{24,28},{28,32},{32,36}... | collective-permute-start | bytes 1179656 | tf_op jit(solution)/shard_map/ppermute | solution.py:25
  7.0 1.5 %fusion.30 = (bf16[1,1,3,3,96,96]{5,4,3,2,1,0:T(8,128)(2,1)S(1)}, bf16[1,1,3,3,96,96]{5,4,3,2,1,0:T(8,128)(2,1)S(1)}, bf16[1,1,3,3,96,96]{5,4,3,2,1,0:T(8,128)(2...) fusion(bf16[2,3,3,3,96,96]{5,4,3,2,1,0:T(8,128)(2,1)} %param.6), kind=kLoop, calls=%fused_computation.111 | loop fusion | bytes 1990656 | tf_op jit(solution)/shard_map/slice | solution.py:57
  8.5 21.3 %collective-permute-done = bf16[2,8,96,128]{3,2,1,0:T(8,128)(2,1)S(1)} collective-permute-done((bf16[2,8,96,128]{3,2,1,0:T(8,128)(2,1)S(1)}, bf16[2,8,96,128]{3,2,1,0:T(8,128)(2,1)S(1)}, u32[]{:S(2)}, u32[]{:S(2)}) %collective-permute-start) | collective-permute-done | bytes 393248 | tf_op jit(solution)/shard_map/ppermute | solution.py:25
  29.8 4.3 %collective-permute-start.1 = (bf16[6,1,96,128]{3,2,1,0:T(8,128)(2,1)S(1)}, bf16[6,1,96,128]{3,2,1,0:T(8,128)(2,1)S(1)}, u32[]{:S(2)}, u32[]{:S(2)}) collective-permute-start(bf16[6,1,96,128]{3,2,1,0:T(8,128)(2,1)S(1)} %get-tuple-element.69), channel_id=1, source_target_pairs={{0,1},{1,2},{2,3},{4,5},{5,6},{6,7},{8,9},{9,10},{10,11},{12,13},{... | collective-permute-start | bytes 442376 | tf_op jit(solution)/shard_map/ppermute | solution.py:16
  34.1 1.9 %collective-permute-start.2 = (bf16[6,1,96,128]{3,2,1,0:T(8,128)(2,1)S(1)}, bf16[6,1,96,128]{3,2,1,0:T(8,128)(2,1)S(1)}, u32[]{:S(2)}, u32[]{:S(2)}) collective-permute-start(bf16[6,1,96,128]{3,2,1,0:T(8,128)(2,1)S(1)} %get-tuple-element.70), channel_id=1, source_target_pairs={{1,0},{2,1},{3,2},{5,4},{6,5},{7,6},{9,8},{10,9},{11,10},{13,12},{... | collective-permute-start | bytes 442376 | tf_op jit(solution)/shard_map/ppermute | solution.py:17
  36.2 4.4 %collective-permute-done.2 = bf16[6,1,96,128]{3,2,1,0:T(8,128)(2,1)S(1)} collective-permute-done((bf16[6,1,96,128]{3,2,1,0:T(8,128)(2,1)S(1)}, bf16[6,1,96,128]{3,2,1,0:T(8,128)(2,1)S(1)}, u32[]{:S(2)}, u32[]{:S(2)}) %collective-permute-start.2) | collective-permute-done | bytes 147488 | tf_op jit(solution)/shard_map/ppermute | solution.py:17
  40.6 2.3 %fusion.8 = bf16[6,10,96,130]{3,2,1,0:T(8,128)(2,1)S(1)} fusion(bf16[6,1,96,128]{3,2,1,0:T(8,128)(2,1)S(1)} %collective-permute-done.2, bf16[6,1,96,128]{3,2,1,0:T(8,128)(2,1)S(1)} %collective-permute-done.1, bf16[4,8,96,128]{3,2,1,0:T(8,128)(2,1)S(1)} %fusion.18, bf16[2,8,96,128]{3,2,1,0:T(8,128)(2,1)S(1)} %collective-permute-done), kind=kLoop, calls=%fused_computation.12 | loop fusion | flops 11232000 | bytes 2972160 | tf_op jit(solution)/shard_map/concatenate | solution.py:18
  44.1 1.1 %slice_dynamic-update-slice_fusion.29 = (bf16[4,8,864,128]{3,2,1,0:T(8,128)(2,1)S(1)}, bf16[4,8,864,128]{3,2,1,0:T(8,128)(2,1)S(1)}, bf16[4,8,864,128]{3,2,1,0:T(8,128)(2,1)S(1)}) fusion(bf16[4,8,864,128]{3,2,1,0:T(8,128)(2,1)S(1)} %get-tuple-element.56, bf16[6,10,96,130]{3,2,1,0:T(8,128)(2,1)S(1)} %fusion.8, ...), kind=kLoop, calls=%fused_computation.78 | loop fusion | bytes 4718592
  45.3 0.6 slice_dynamic-update-slice_fusion.28
  46.4 1.1 %slice_dynamic-update-slice_fusion.27 = (bf16[4,8,864,128]{3,2,1,0:T(8,128)(2,1)S(1)}, bf16[4,8,864,128]{3,2,1,0:T(8,128)(2,1)S(1)}, bf16[4,8,864,128]{3,2,1,0:T(8,128)(2,1)S(1)}) fusion(bf16[4,8,864,128]{3,2,1,0:T(8,128)(2,1)S(1)} %get-tuple-element.72, bf16[6,10,96,130]{3,2,1,0:T(8,128)(2,1)S(1)} %fusion.8, ...), kind=kLoop, calls=%fused_computation.76 | loop fusion | bytes 4718592
  47.5 0.6 slice_dynamic-update-slice_fusion.26
  48.7 1.1 %slice_dynamic-update-slice_fusion.24 = (bf16[4,8,864,128]{3,2,1,0:T(8,128)(2,1)S(1)}, bf16[4,8,864,128]{3,2,1,0:T(8,128)(2,1)S(1)}, bf16[4,8,864,128]{3,2,1,0:T(8,128)(2,1)S(1)}) fusion(bf16[4,8,864,128]{3,2,1,0:T(8,128)(2,1)S(1)} %get-tuple-element.53, bf16[6,10,96,130]{3,2,1,0:T(8,128)(2,1)S(1)} %fusion.8, ...), kind=kLoop, calls=%fused_computation.73 | loop fusion | bytes 4718592 | tf_op jit(solution)/shard_map/concatenate | solution.py:44
  49.8 1.4 %fusion.31 = f32[4,8,128,96]{2,3,1,0:T(8,128)S(1)} fusion(bf16[4,8,864,128]{3,2,1,0:T(8,128)(2,1)S(1)} %get-tuple-element.25, bf16[864,96,1,1]{1,0,3,2:T(8,128)(2,1)S(1)} %bitcast.56), kind=kOutput, calls=%fused_computation.112 | convolution fusion | flops 679477248 | bytes 8816640 | tf_op jit(solution)/shard_map/trkw,ko->trow/dot_general | solution.py:54
  51.2 1.4 %fusion.32 = f32[4,8,128,96]{2,3,1,0:T(8,128)S(1)} fusion(bf16[4,8,864,128]{3,2,1,0:T(8,128)(2,1)S(1)} %get-tuple-element.24, bf16[864,96,1,1]{1,0,3,2:T(8,128)(2,1)S(1)} %bitcast.55), kind=kOutput, calls=%fused_computation.113 | convolution fusion | flops 679477248 | bytes 8816640 | tf_op jit(solution)/shard_map/trkw,ko->trow/dot_general | solution.py:54
  52.6 1.5 %multiply_reduce_fusion = (f32[4,8,128]{2,1,0:T(8,128)S(1)}, f32[4,8,128,96]{2,3,1,0:T(8,128)S(1)}) fusion(f32[96]{0:T(128)S(1)} %get-tuple-element.74, bf16[4,8,864,128]{3,2,1,0:T(8,128)(2,1)S(1)} %get-tuple-element.23, bf16[864,96,1,1]{1,0,3,2:T(8,128)(2,1)S(1)} %bitcast.58, f32[4,8,128,96]{2,3,1,0:T(8,128)S(1)} %fusion.31, f32[4,8,128,96]{2,3,1,0:T(8,128)S(1)} %fusion.32), kind=kOutput, calls=%fused_computation.32 | convolution fusion | flops 681439232 | bytes 11979136 | tf_op jit(solution)/shard_map/trkw,ko->trow/dot_general | solution.py:54
  54.8 1.9 %collective-permute-start.3 = (bf16[2,8,96,128]{3,2,1,0:T(8,128)(2,1)S(1)}, bf16[2,8,96,128]{3,2,1,0:T(8,128)(2,1)S(1)}, u32[]{:S(2)}, u32[]{:S(2)}) collective-permute-start(bf16[2,8,96,128]{3,2,1,0:T(8,128)(2,1)S(1)} %slice.351), channel_id=1, source_target_pairs={{0,4},{4,8},{8,12},{12,16},{16,20},{20,24},{24,28},{28,32},{32,36}... | collective-permute-start | bytes 1179656 | tf_op jit(solution)/shard_map/ppermute | solution.py:25
  56.7 21.0 %collective-permute-done.3 = bf16[2,8,96,128]{3,2,1,0:T(8,128)(2,1)S(1)} collective-permute-done((bf16[2,8,96,128]{3,2,1,0:T(8,128)(2,1)S(1)}, bf16[2,8,96,128]{3,2,1,0:T(8,128)(2,1)S(1)}, u32[]{:S(2)}, u32[]{:S(2)}) %collective-permute-start.3) | collective-permute-done | bytes 393248 | tf_op jit(solution)/shard_map/ppermute | solution.py:25
  77.7 2.6 %collective-permute-start.4 = (bf16[6,1,96,128]{3,2,1,0:T(8,128)(2,1)S(1)}, bf16[6,1,96,128]{3,2,1,0:T(8,128)(2,1)S(1)}, u32[]{:S(2)}, u32[]{:S(2)}) collective-permute-start(bf16[6,1,96,128]{3,2,1,0:T(8,128)(2,1)S(1)} %get-tuple-element.63), channel_id=1, source_target_pairs={{0,1},{1,2},{2,3},{4,5},{5,6},{6,7},{8,9},{9,10},{10,11},{12,13},{... | collective-permute-start | bytes 442376 | tf_op jit(solution)/shard_map/ppermute | solution.py:16
  80.3 2.1 %collective-permute-start.5 = (bf16[6,1,96,128]{3,2,1,0:T(8,128)(2,1)S(1)}, bf16[6,1,96,128]{3,2,1,0:T(8,128)(2,1)S(1)}, u32[]{:S(2)}, u32[]{:S(2)}) collective-permute-start(bf16[6,1,96,128]{3,2,1,0:T(8,128)(2,1)S(1)} %get-tuple-element.64), channel_id=1, source_target_pairs={{1,0},{2,1},{3,2},{5,4},{6,5},{7,6},{9,8},{10,9},{11,10},{13,12},{... | collective-permute-start | bytes 442376 | tf_op jit(solution)/shard_map/ppermute | solution.py:17
  82.5 4.3 %collective-permute-done.5 = bf16[6,1,96,128]{3,2,1,0:T(8,128)(2,1)S(1)} collective-permute-done((bf16[6,1,96,128]{3,2,1,0:T(8,128)(2,1)S(1)}, bf16[6,1,96,128]{3,2,1,0:T(8,128)(2,1)S(1)}, u32[]{:S(2)}, u32[]{:S(2)}) %collective-permute-start.5) | collective-permute-done | bytes 147488 | tf_op jit(solution)/shard_map/ppermute | solution.py:17
  86.8 2.3 %select_maximum_fusion = bf16[6,10,96,130]{3,2,1,0:T(8,128)(2,1)S(1)} fusion(bf16[6,1,96,128]{3,2,1,0:T(8,128)(2,1)S(1)} %collective-permute-done.5, bf16[6,1,96,128]{3,2,1,0:T(8,128)(2,1)S(1)} %collective-permute-done.4, bf16[4,8,96,128]{3,2,1,0:T(8,128)(2,1)S(1)} %fusion.23, bf16[2,8,96,128]{3,2,1,0:T(8,128)(2,1)S(1)} %collective-permute-done.3), kind=kLoop, calls=%fused_computation.3 | loop fusion | flops 11232000 | bytes 2972160 | tf_op jit(solution)/shard_map/concatenate | solution.py:18
  90.3 1.1 %slice_dynamic-update-slice_fusion.5 = (bf16[4,8,864,128]{3,2,1,0:T(8,128)(2,1)S(1)}, bf16[4,8,864,128]{3,2,1,0:T(8,128)(2,1)S(1)}, bf16[4,8,864,128]{3,2,1,0:T(8,128)(2,1)S(1)}) fusion(bf16[4,8,864,128]{3,2,1,0:T(8,128)(2,1)S(1)} %get-tuple-element.50, bf16[6,10,96,130]{3,2,1,0:T(8,128)(2,1)S(1)} %select_maximum_fusion, ...), kind=kLoop, calls=%fused_computation.52 | loop fusion | bytes 4718592
  91.5 0.6 slice_dynamic-update-slice_fusion.4
  92.6 1.1 %slice_dynamic-update-slice_fusion.3 = (bf16[4,8,864,128]{3,2,1,0:T(8,128)(2,1)S(1)}, bf16[4,8,864,128]{3,2,1,0:T(8,128)(2,1)S(1)}, bf16[4,8,864,128]{3,2,1,0:T(8,128)(2,1)S(1)}) fusion(bf16[4,8,864,128]{3,2,1,0:T(8,128)(2,1)S(1)} %get-tuple-element.71, bf16[6,10,96,130]{3,2,1,0:T(8,128)(2,1)S(1)} %select_maximum_fusion, ...), kind=kLoop, calls=%fused_computation.50 | loop fusion | bytes 4718592
  93.7 0.6 slice_dynamic-update-slice_fusion.2
  94.9 1.1 %slice_dynamic-update-slice_fusion = (bf16[4,8,864,128]{3,2,1,0:T(8,128)(2,1)S(1)}, bf16[4,8,864,128]{3,2,1,0:T(8,128)(2,1)S(1)}, bf16[4,8,864,128]{3,2,1,0:T(8,128)(2,1)S(1)}) fusion(bf16[4,8,864,128]{3,2,1,0:T(8,128)(2,1)S(1)} %get-tuple-element.47, bf16[6,10,96,130]{3,2,1,0:T(8,128)(2,1)S(1)} %select_maximum_fusion, ...), kind=kLoop, calls=%fused_computation.47 | loop fusion | bytes 4718592 | tf_op jit(solution)/shard_map/concatenate | solution.py:44
  96.0 1.4 %fusion.34 = f32[4,8,128,96]{2,3,1,0:T(8,128)S(1)} fusion(bf16[4,8,864,128]{3,2,1,0:T(8,128)(2,1)S(1)} %get-tuple-element.6, bf16[864,96,1,1]{1,0,3,2:T(8,128)(2,1)S(1)} %bitcast.54), kind=kOutput, calls=%fused_computation.115 | convolution fusion | flops 679477248 | bytes 8816640 | tf_op jit(solution)/shard_map/trkw,ko->trow/dot_general | solution.py:54
  97.4 1.4 %fusion.33 = f32[4,8,128,96]{2,3,1,0:T(8,128)S(1)} fusion(bf16[4,8,864,128]{3,2,1,0:T(8,128)(2,1)S(1)} %get-tuple-element.7, bf16[864,96,1,1]{1,0,3,2:T(8,128)(2,1)S(1)} %bitcast.53), kind=kOutput, calls=%fused_computation.114 | convolution fusion | flops 679477248 | bytes 8816640 | tf_op jit(solution)/shard_map/trkw,ko->trow/dot_general | solution.py:54
  98.8 2.5 %fusion.19 = bf16[4,8,96,128]{3,2,1,0:T(8,128)(2,1)} fusion(bf16[4,8,96,128]{3,2,1,0:T(8,128)(2,1)S(1)} %copy-done, f32[4,8,128,96]{2,3,1,0:T(8,128)S(1)} %fusion.33, f32[4,8,128,96]{2,3,1,0:T(8,128)S(1)} %fusion.34, bf16[4,8,864,128]{3,2,1,0:T(8,128)(2,1)S(1)} %get-tuple-element.5, bf16[864,96,1,1]{1,0,3,2:T(8,128)(2,1)S(1)} %bitcast.57, ...), kind=kOutput, calls=%fused_computation.26 | convolution fusion | flops 681836544 | bytes 11962752 | tf_op jit(solution)/shard_map/trkw,ko->trow/dot_general | solution.py:54
  (24 shorter events, 5.3 us)
Async XLA Ops:
  0.0 36.1 %copy-start.1 = (f32[2,96]{1,0:T(2,128)S(1)}, f32[2,96]{1,0:T(2,128)}, u32[]{:S(2)}) copy-start(f32[2,96]{1,0:T(2,128)} %param.7) | copy-start | bytes 2308
  3.8 26.0 %collective-permute-start = (bf16[2,8,96,128]{3,2,1,0:T(8,128)(2,1)S(1)}, bf16[2,8,96,128]{3,2,1,0:T(8,128)(2,1)S(1)}, u32[]{:S(2)}, u32[]{:S(2)}) collective-permute-start(bf16[2,8,96,128]{3,2,1,0:T(8,128)(2,1)S(1)} %slice.324), channel_id=1, source_target_pairs={{0,4},{4,8},{8,12},{12,16},{16,20},{20,24},{24,28},{28,32},{32,36}... | collective-permute-start | bytes 1179656 | tf_op jit(solution)/shard_map/ppermute | solution.py:25
  29.8 6.4 %collective-permute-start.1 = (bf16[6,1,96,128]{3,2,1,0:T(8,128)(2,1)S(1)}, bf16[6,1,96,128]{3,2,1,0:T(8,128)(2,1)S(1)}, u32[]{:S(2)}, u32[]{:S(2)}) collective-permute-start(bf16[6,1,96,128]{3,2,1,0:T(8,128)(2,1)S(1)} %get-tuple-element.69), channel_id=1, source_target_pairs={{0,1},{1,2},{2,3},{4,5},{5,6},{6,7},{8,9},{9,10},{10,11},{12,13},{... | collective-permute-start | bytes 442376 | tf_op jit(solution)/shard_map/ppermute | solution.py:16
  34.1 6.5 %collective-permute-start.2 = (bf16[6,1,96,128]{3,2,1,0:T(8,128)(2,1)S(1)}, bf16[6,1,96,128]{3,2,1,0:T(8,128)(2,1)S(1)}, u32[]{:S(2)}, u32[]{:S(2)}) collective-permute-start(bf16[6,1,96,128]{3,2,1,0:T(8,128)(2,1)S(1)} %get-tuple-element.70), channel_id=1, source_target_pairs={{1,0},{2,1},{3,2},{5,4},{6,5},{7,6},{9,8},{10,9},{11,10},{13,12},{... | collective-permute-start | bytes 442376 | tf_op jit(solution)/shard_map/ppermute | solution.py:17
  54.8 22.9 %collective-permute-start.3 = (bf16[2,8,96,128]{3,2,1,0:T(8,128)(2,1)S(1)}, bf16[2,8,96,128]{3,2,1,0:T(8,128)(2,1)S(1)}, u32[]{:S(2)}, u32[]{:S(2)}) collective-permute-start(bf16[2,8,96,128]{3,2,1,0:T(8,128)(2,1)S(1)} %slice.351), channel_id=1, source_target_pairs={{0,4},{4,8},{8,12},{12,16},{16,20},{20,24},{24,28},{28,32},{32,36}... | collective-permute-start | bytes 1179656 | tf_op jit(solution)/shard_map/ppermute | solution.py:25
  77.7 4.7 %collective-permute-start.4 = (bf16[6,1,96,128]{3,2,1,0:T(8,128)(2,1)S(1)}, bf16[6,1,96,128]{3,2,1,0:T(8,128)(2,1)S(1)}, u32[]{:S(2)}, u32[]{:S(2)}) collective-permute-start(bf16[6,1,96,128]{3,2,1,0:T(8,128)(2,1)S(1)} %get-tuple-element.63), channel_id=1, source_target_pairs={{0,1},{1,2},{2,3},{4,5},{5,6},{6,7},{8,9},{9,10},{10,11},{12,13},{... | collective-permute-start | bytes 442376 | tf_op jit(solution)/shard_map/ppermute | solution.py:16
  80.3 6.5 %collective-permute-start.5 = (bf16[6,1,96,128]{3,2,1,0:T(8,128)(2,1)S(1)}, bf16[6,1,96,128]{3,2,1,0:T(8,128)(2,1)S(1)}, u32[]{:S(2)}, u32[]{:S(2)}) collective-permute-start(bf16[6,1,96,128]{3,2,1,0:T(8,128)(2,1)S(1)} %get-tuple-element.64), channel_id=1, source_target_pairs={{1,0},{2,1},{3,2},{5,4},{6,5},{7,6},{9,8},{10,9},{11,10},{13,12},{... | collective-permute-start | bytes 442376 | tf_op jit(solution)/shard_map/ppermute | solution.py:17
  96.0 2.8 %copy-start = (bf16[4,8,96,128]{3,2,1,0:T(8,128)(2,1)S(1)}, bf16[4,8,96,128]{3,2,1,0:T(8,128)(2,1)}, u32[]{:S(2)}) copy-start(bf16[4,8,96,128]{3,2,1,0:T(8,128)(2,1)} %param.4) | copy-start | bytes 2359300
where the time goes:
time: 102 us; the launch traced here: 101 us
  waiting for transfers between devices  51.1 us (50%)
  starting transfers between devices  16 us (16%)
  local copies, waits for them, and re-layouts  14.5 us (14%)
  other arithmetic  9.72 us (10%)
  matrix products  9.59 us (9%)
    ppermute x2, waiting for transfers between devices, shifted(): return lax.ppermute(block, axis, route)  42.3 us
    unnamed x18, local copies, waits for them, and re-layouts  9.85 us
    dot_general x6, matrix products, valid_conv(): jnp.einsum('trkw,ko->trow', stacked, kernel[tap_t].reshape(9 * channels,...  9.59 us
    ppermute x2, waiting for transfers between devices, with_halo(): after = lax.ppermute(first, axis, down)  8.72 us
    ppermute x2, starting transfers between devices, with_halo(): before = lax.ppermute(last, axis, up)  6.9 us
    ppermute x2, starting transfers between devices, shifted(): return lax.ppermute(block, axis, route)  5.13 us
    concatenate x4, other arithmetic, with_halo(): x = jnp.concatenate([before, x, after], axis=dim)  5.03 us
    ppermute x2, starting transfers between devices, with_halo(): after = lax.ppermute(first, axis, down)  4.02 us
  transfers between devices with their start and end apart: 6, of which 5 were waited for; matrix products, arithmetic and copies ran while one was open for 1% of the time, Pallas kernels for 0%

commit v1 on v0

v1 whole, which is shorter than its diff:
```python
import functools

import jax
import jax.numpy as jnp
from jax import lax
from jax.experimental import pallas as pl
from jax.experimental.pallas import tpu as pltpu
from jax.sharding import PartitionSpec as P

EPS = 1e-06
VMEM_BYTES = 48 * 1024 * 1024
F32 = jnp.float32
BF16 = jnp.bfloat16


def activated(values, gain):
    mean_sq = jnp.mean(values * values, axis=0, keepdims=True)
    half = values * lax.rsqrt(mean_sq + EPS) * (0.5 * gain)
    return half + half * jnp.tanh(half)


def store_taps(ref, frame, row, act):
    channels, cols = act.shape
    lane = lax.broadcasted_iota(jnp.int32, act.shape, 1)
    left = jnp.where(lane == 0, 0.0, pltpu.roll(act, 1, 1))
    right = jnp.where(lane == cols - 1, 0.0, pltpu.roll(act, cols - 1, 1))
    ref[frame, row, 0:channels] = left.astype(BF16)
    ref[frame, row, channels : 2 * channels] = act.astype(BF16)
    ref[frame, row, 2 * channels :] = right.astype(BF16)


def row_pair(ref, frame, row):
    depth, cols = ref.shape[2], ref.shape[3]
    first = ref[frame, row : row + 3].reshape(3 * depth, cols)
    second = ref[frame, row + 1 : row + 4].reshape(3 * depth, cols)
    return jnp.concatenate([first, second], axis=1)


def tap_products(weights_ref, index, taps, columns):
    channels = weights_ref.shape[1] // 3
    low, high = taps
    product = jnp.dot(
        weights_ref[index, low * channels : (high + 1) * channels],
        columns,
        preferred_element_type=F32,
    )
    return {
        tap: product[(tap - low) * channels : (tap - low + 1) * channels]
        for tap in range(low, high + 1)
    }


def prepare_kernel(kernels_ref, gains_ref, biases_ref, weights_ref, gain_ref, bias_ref):
    channels = gains_ref.shape[1]
    cols = gain_ref.shape[2]
    for index in range(2):
        for tap in range(3):
            weights_ref[index, tap * channels : (tap + 1) * channels, :] = kernels_ref[index, tap].T
        for source, target in ((gains_ref, gain_ref), (biases_ref, bias_ref)):
            spread = jnp.broadcast_to(source[index : index + 1], (cols, channels))
            target[index] = spread.T


def halves(pair):
    cols = pair.shape[1] // 2
    return pair[:, :cols], pair[:, cols:]


def local_kernel(
    stream_ref, above_ref, below_ref, weights_ref, gain_ref, bias_ref,
    send_ref, hidden_ref, base_ref,
    taps_ref, normed_ref,
):
    frames, rows = stream_ref.shape[:2]
    band = lax.axis_index("rows")
    keep_above = jnp.where(band > 0, 1.0, 0.0)
    keep_below = jnp.where(band < lax.axis_size("rows") - 1, 1.0, 0.0)
    gain = gain_ref[0]
    for frame in range(frames):
        for row in range(rows + 4):
            if row < 2:
                values = above_ref[frame, row]
            elif row < rows + 2:
                values = stream_ref[frame, row - 2]
            else:
                values = below_ref[frame, row - rows - 2]
            store_taps(taps_ref, frame, row, activated(values.astype(F32), gain))
    gain = gain_ref[1]
    bias = jnp.concatenate([bias_ref[0]] * 2, axis=1)
    for pair in range((rows + 2) // 2):
        y = [
            tap_products(weights_ref, 0, taps, row_pair(taps_ref, frame, 2 * pair))
            for frame, taps in enumerate(((0, 2), (0, 2), (1, 2), (2, 2)))
        ]
        hidden = [
            y[0][2] + bias,
            y[0][1] + y[1][2] + bias,
            y[0][0] + y[1][1] + y[2][2] + bias,
            y[1][0] + y[2][1] + y[3][2] + bias,
        ]
        for frame in range(4):
            for side, values in enumerate(halves(hidden[frame])):
                row = 2 * pair + side
                if frame < 2:
                    hidden_ref[frame, row] = values
                    continue
                act = activated(values, gain)
                if row == 0:
                    act = act * keep_above
                if row == rows + 1:
                    act = act * keep_below
                store_taps(normed_ref, frame - 2, row, act)
    bias = bias_ref[1]
    for pair in range(rows // 2):
        y2 = tap_products(weights_ref, 1, (0, 2), row_pair(normed_ref, 0, 2 * pair))
        y3 = tap_products(weights_ref, 1, (0, 2), row_pair(normed_ref, 1, 2 * pair))
        for side in range(2):
            row = 2 * pair + side
            send_ref[0, row] = (halves(y2[0])[side] + halves(y3[1])[side]).astype(BF16)
            send_ref[1, row] = halves(y3[0])[side].astype(BF16)
            base_ref[0, row] = halves(y2[2])[side] + bias + stream_ref[2, row].astype(F32)
            base_ref[1, row] = (
                halves(y2[1])[side] + halves(y3[2])[side] + bias + stream_ref[3, row].astype(F32)
            )


def history_kernel(
    earlier_ref, above_ref, below_ref, hidden_ref, base_ref, stream_ref, weights_ref, gain_ref, bias_ref,
    out_ref, first_ref,
    taps_ref, normed_ref,
):
    rows = earlier_ref.shape[1]
    band = lax.axis_index("rows")
    keep_above = jnp.where(band > 0, 1.0, 0.0)
    keep_below = jnp.where(band < lax.axis_size("rows") - 1, 1.0, 0.0)
    gain = gain_ref[0]
    for frame in range(2):
        for row in range(rows + 4):
            if row < 2:
                values = above_ref[frame, row]
            elif row < rows + 2:
                values = earlier_ref[frame, row - 2]
            else:
                values = below_ref[frame, row - rows - 2]
            store_taps(taps_ref, frame, row, activated(values.astype(F32), gain))
    gain = gain_ref[1]
    for pair in range((rows + 2) // 2):
        y0 = tap_products(weights_ref, 0, (0, 0), row_pair(taps_ref, 0, 2 * pair))
        y1 = tap_products(weights_ref, 0, (0, 1), row_pair(taps_ref, 1, 2 * pair))
        hidden = [y0[0] + y1[1], y1[0]]
        for frame in range(2):
            for side, values in enumerate(halves(hidden[frame])):
                row = 2 * pair + side
                act = activated(values + hidden_ref[frame, row], gain)
                if row == 0:
                    act = act * keep_above
                if row == rows + 1:
                    act = act * keep_below
                store_taps(normed_ref, frame, row, act)
    bias = bias_ref[1]
    for pair in range(rows // 2):
        y0 = tap_products(weights_ref, 1, (0, 2), row_pair(normed_ref, 0, 2 * pair))
        y1 = tap_products(weights_ref, 1, (0, 2), row_pair(normed_ref, 1, 2 * pair))
        for side in range(2):
            row = 2 * pair + side
            first_ref[0, row] = halves(y0[2])[side] + bias + stream_ref[0, row].astype(F32)
            first_ref[1, row] = (
                halves(y0[1])[side] + halves(y1[2])[side] + bias + stream_ref[1, row].astype(F32)
            )
            out_ref[2, row] = (
                base_ref[0, row] + halves(y0[0])[side] + halves(y1[1])[side]
            ).astype(BF16)
            out_ref[3, row] = (base_ref[1, row] + halves(y1[0])[side]).astype(BF16)


def finish_kernel(partial_ref, first_ref, _, out_ref):
    out_ref[...] = (first_ref[...] + partial_ref[...].astype(F32)).astype(BF16)


def call(kernel, outs, scratch=(), flops=0, moved=0):
    return pl.pallas_call(
        kernel,
        out_shape=[jax.ShapeDtypeStruct(*out) for out in outs],
        scratch_shapes=list(scratch),
        compiler_params=pltpu.CompilerParams(vmem_limit_bytes=VMEM_BYTES),
        cost_estimate=pl.CostEstimate(flops=flops, bytes_accessed=moved, transcendentals=0),
    )


def steps(axis, distance):
    size = lax.axis_size(axis)
    return [(i, i + distance) for i in range(size) if 0 <= i + distance < size]


def row_edges(block):
    rows = block.shape[1]
    above = lax.ppermute(block[:, rows - 2 :], "rows", steps("rows", 1))
    below = lax.ppermute(block[:, :2], "rows", steps("rows", -1))
    return above, below


def shards(stream, gains, kernels, biases):
    frames, rows, channels, cols = stream.shape
    plane = (channels, cols)
    cells = rows * cols
    mac = 2 * 9 * channels * channels
    earlier = lax.ppermute(stream[frames - 2 :], "tm", steps("tm", 1))
    above, below = row_edges(stream)
    weights, gain, bias = call(
        prepare_kernel,
        [
            ((2, 3 * channels, 9 * channels), BF16),
            ((2, *plane), F32),
            ((2, *plane), F32),
        ],
        flops=10**6,
        moved=4 * 10**6,
    )(kernels.reshape(2, 3, 9 * channels, channels), gains, biases)
    sent, hidden, base = call(
        local_kernel,
        [
            ((2, rows, *plane), BF16),
            ((2, rows + 2, *plane), F32),
            ((2, rows, *plane), F32),
        ],
        [
            pltpu.VMEM((frames, rows + 4, 3 * channels, cols), BF16),
            pltpu.VMEM((2, rows + 2, 3 * channels, cols), BF16),
        ],
        flops=mac * cells * 18,
        moved=4 * 10**6,
    )(stream, above, below, weights, gain, bias)
    partial = lax.ppermute(sent, "tm", steps("tm", 1))
    above, below = row_edges(earlier)
    out, first = call(
        history_kernel,
        [((frames, rows, *plane), BF16), ((2, rows, *plane), F32)],
        [
            pltpu.VMEM((2, rows + 4, 3 * channels, cols), BF16),
            pltpu.VMEM((2, rows + 2, 3 * channels, cols), BF16),
        ],
        flops=mac * cells * 10,
        moved=4 * 10**6,
    )(earlier, above, below, hidden, base, stream, weights, gain, bias)
    block = pl.BlockSpec((2, rows, *plane), lambda i: (0, 0, 0, 0))
    return pl.pallas_call(
        finish_kernel,
        grid=(1,),
        out_shape=jax.ShapeDtypeStruct(stream.shape, BF16),
        in_specs=[block, block, pl.BlockSpec(memory_space=pl.ANY)],
        out_specs=block,
        input_output_aliases={2: 0},
        compiler_params=pltpu.CompilerParams(vmem_limit_bytes=VMEM_BYTES),
        cost_estimate=pl.CostEstimate(flops=10**6, bytes_accessed=2 * 10**6, transcendentals=0),
    )(partial, first, out)


def solution(mesh):
    placed = (P("tm", "rows", None, None), P(), P(), P())
    return jax.shard_map(
        shards, mesh=mesh, in_specs=placed, out_specs=P("tm", "rows", None, None), check_vma=False
    )
```

time: 102 us -> 54.3 us (0.53)
  the two profiles are of different devices: /device:TPU:257 before, /device:TPU:135 now
where the time goes in v1:
time: 54.3 us; the launch traced here: 54 us
  waiting for transfers between devices  21.7 us (40%)
  starting transfers between devices  19.7 us (36%)
  Pallas kernels  8.86 us (16%)
  local copies, waits for them, and re-layouts  3.6 us (7%)
    ppermute x2, waiting for transfers between devices, row_edges(): above = lax.ppermute(block[:, rows - 2:], 'rows', steps('rows', 1))  21.7 us
    ppermute x2, starting transfers between devices, row_edges(): above = lax.ppermute(block[:, rows - 2:], 'rows', steps('rows', 1))  9.47 us
    pallas_call x1, Pallas kernels, shards(): call(local_kernel, [((2, rows, *plane), BF16), ((2, rows + 2, *plane), F3...  4.2 us
    ppermute x2, starting transfers between devices, row_edges(): below = lax.ppermute(block[:, :2], 'rows', steps('rows', -1))  3.84 us
    pallas_call x1, Pallas kernels, shards(): call(history_kernel, [((frames, rows, *plane), BF16), ((2, rows, *plane),...  3.36 us
    ppermute x1, starting transfers between devices, shards(): partial = lax.ppermute(sent, 'tm', steps('tm', 1))  3.21 us
    ppermute x1, starting transfers between devices, shards(): earlier = lax.ppermute(stream[frames - 2:], 'tm', steps('tm', 1))  3.2 us
    unnamed x8, local copies, waits for them, and re-layouts  1.36 us
  transfers between devices with their start and end apart: 6, of which 1 were waited for; matrix products, arithmetic and copies ran while one was open for 2% of the time, Pallas kernels for 15%

profile of v1, /device:TPU:135, one launch (start us, length us, event | category | flops | bytes accessed | tf_op | source)
XLA Modules:
  0.0 54.0 jit_solution(1564607343288964837)
XLA Ops:
  0.0 0.0 copy-start
  0.0 0.0 copy-start.1
  0.0 1.2 %fusion = (bf16[4,2,96,128]{3,2,1,0:T(8,128)(2,1)S(1)}, bf16[4,2,96,128]{3,2,1,0:T(8,128)(2,1)S(1)}) fusion(bf16[4,8,96,128]{3,2,1,0:T(8,128)(2,1)} %stream_ref.3), kind=kLoop, calls=%fused_computation | loop fusion | bytes 786432 | tf_op jit(solution)/shard_map/slice | solution.py:198
  1.2 4.6 %collective-permute-start = (bf16[4,2,96,128]{3,2,1,0:T(8,128)(2,1)S(1)}, bf16[4,2,96,128]{3,2,1,0:T(8,128)(2,1)S(1)}, u32[]{:S(2)}, u32[]{:S(2)}) collective-permute-start(bf16[4,2,96,128]{3,2,1,0:T(8,128)(2,1)S(1)} %get-tuple-element.22), channel_id=1, source_target_pairs={{0,1},{1,2},{2,3},{4,5},{5,6},{6,7},{8,9},{9,10},{10,11},{12,13},{... | collective-permute-start | bytes 589832 | tf_op jit(solution)/shard_map/ppermute | solution.py:197
  5.8 1.9 %collective-permute-start.1 = (bf16[4,2,96,128]{3,2,1,0:T(8,128)(2,1)S(1)}, bf16[4,2,96,128]{3,2,1,0:T(8,128)(2,1)S(1)}, u32[]{:S(2)}, u32[]{:S(2)}) collective-permute-start(bf16[4,2,96,128]{3,2,1,0:T(8,128)(2,1)S(1)} %get-tuple-element.21), channel_id=1, source_target_pairs={{1,0},{2,1},{3,2},{5,4},{6,5},{7,6},{9,8},{10,9},{11,10},{13,12},{... | collective-permute-start | bytes 589832 | tf_op jit(solution)/shard_map/ppermute | solution.py:198
  7.7 1.0 %slice.17 = bf16[2,8,96,128]{3,2,1,0:T(8,128)(2,1)S(1)} slice(bf16[4,8,96,128]{3,2,1,0:T(8,128)(2,1)} %stream_ref.3), slice={[2:4], [0:8], [0:96], [0:128]} | slice | bytes 786432 | tf_op jit(solution)/shard_map/slice | solution.py:207
  8.7 3.2 %collective-permute-start.3 = (bf16[2,8,96,128]{3,2,1,0:T(8,128)(2,1)S(1)}, bf16[2,8,96,128]{3,2,1,0:T(8,128)(2,1)S(1)}, u32[]{:S(2)}, u32[]{:S(2)}) collective-permute-start(bf16[2,8,96,128]{3,2,1,0:T(8,128)(2,1)S(1)} %slice.17), channel_id=1, source_target_pairs={{0,4},{4,8},{8,12},{12,16},{16,20},{20,24},{24,28},{28,32},{32,36}... | collective-permute-start | bytes 1179656 | tf_op jit(solution)/shard_map/ppermute | solution.py:207
  11.9 0.0 copy-done
  12.0 0.0 copy-start.2
  12.0 0.7 %copy-done.2 = f32[2,96]{1,0:T(2,128)S(1)} copy-done((f32[2,96]{1,0:T(2,128)S(1)}, f32[2,96]{1,0:T(2,128)}, u32[]{:S(2)}) %copy-start.2) | copy-done | bytes 792
  12.6 0.0 copy-start.3
  12.6 0.7 %copy-done.3 = f32[2,96]{1,0:T(2,128)S(1)} copy-done((f32[2,96]{1,0:T(2,128)S(1)}, f32[2,96]{1,0:T(2,128)}, u32[]{:S(2)}) %copy-start.3) | copy-done | bytes 792
  13.3 0.5 shard_map.46
  13.8 0.0 collective-permute-done.above_ref
  13.8 0.0 collective-permute-done.1.below_ref
  13.8 0.0 copy-done.1
  13.8 4.2 %shard_map.47 = (bf16[2,8,96,128]{3,2,1,0:T(8,128)(2,1)S(1)}, f32[2,10,96,128]{3,2,1,0:T(8,128)S(1)}, f32[2,8,96,128]{3,2,1,0:T(8,128)S(1)}) custom-call(bf16[4,8,96,128]{3,2,1,0:T(8,128)(2,1)S(1)} %copy-done.1, bf16[4,2,96,128]{3,2,1,0:T(8,128)(2,1)S(1)} %collective-permute-done.above_ref, bf16[4,2,96,128]{3,2,1,0:T(8,128)(2,1)S(1)} %collective-permute-done.1.below_ref, ...), custom_call_target="tpu_custom_call" | custom-call | flops 3057647616 | bytes 4000000 | tf_op jit(solution)/shard_map/pallas_call | solution.py:219
  18.0 3.2 %collective-permute-start.2 = (bf16[2,8,96,128]{3,2,1,0:T(8,128)(2,1)S(1)}, bf16[2,8,96,128]{3,2,1,0:T(8,128)(2,1)S(1)}, u32[]{:S(2)}, u32[]{:S(2)}) collective-permute-start(bf16[2,8,96,128]{3,2,1,0:T(8,128)(2,1)S(1)} %get-tuple-element.16), channel_id=1, source_target_pairs={{0,4},{4,8},{8,12},{12,16},{16,20},{20,24},{24,28},{28,32},{32,36}... | collective-permute-start | bytes 1179656 | tf_op jit(solution)/shard_map/ppermute | solution.py:233
  21.3 0.0 collective-permute-done.3.earlier_ref
  21.3 4.9 %collective-permute-start.4 = (bf16[2,2,96,128]{3,2,1,0:T(8,128)(2,1)S(1)}, bf16[2,2,96,128]{3,2,1,0:T(8,128)(2,1)S(1)}, u32[]{:S(2)}, u32[]{:S(2)}) collective-permute-start(bf16[2,2,96,128]{3,2,1,0:T(8,128)(2,1)S(1)} %get-tuple-element.24), channel_id=1, source_target_pairs={{0,1},{1,2},{2,3},{4,5},{5,6},{6,7},{8,9},{9,10},{10,11},{12,13},{... | collective-permute-start | bytes 294920 | tf_op jit(solution)/shard_map/ppermute | solution.py:197
  26.2 1.9 %collective-permute-start.5 = (bf16[2,2,96,128]{3,2,1,0:T(8,128)(2,1)S(1)}, bf16[2,2,96,128]{3,2,1,0:T(8,128)(2,1)S(1)}, u32[]{:S(2)}, u32[]{:S(2)}) collective-permute-start(bf16[2,2,96,128]{3,2,1,0:T(8,128)(2,1)S(1)} %get-tuple-element.23), channel_id=1, source_target_pairs={{1,0},{2,1},{3,2},{5,4},{6,5},{7,6},{9,8},{10,9},{11,10},{13,12},{... | collective-permute-start | bytes 294920 | tf_op jit(solution)/shard_map/ppermute | solution.py:198
  28.1 21.7 %collective-permute-done.4.above_ref = bf16[2,2,96,128]{3,2,1,0:T(8,128)(2,1)S(1)} collective-permute-done((bf16[2,2,96,128]{3,2,1,0:T(8,128)(2,1)S(1)}, bf16[2,2,96,128]{3,2,1,0:T(8,128)(2,1)S(1)}, u32[]{:S(2)}, u32[]{:S(2)}) %collective-permute-start.4) | collective-permute-done | bytes 98336 | tf_op jit(solution)/shard_map/ppermute | solution.py:197
  49.8 0.0 collective-permute-done.5.below_ref
  49.8 3.4 %shard_map.48 = (bf16[4,8,96,128]{3,2,1,0:T(8,128)(2,1)}, f32[2,8,96,128]{3,2,1,0:T(8,128)S(1)}) custom-call(bf16[2,8,96,128]{3,2,1,0:T(8,128)(2,1)S(1)} %collective-permute-done.3.earlier_ref, bf16[2,2,96,128]{3,2,1,0:T(8,128)(2,1)S(1)} %collective-permute-done.4.above_ref, bf16[2,2,96,128]{3,2,1,0:T(8,128)(2,1)S(1)} %collective-permute-done.5.below_ref, ...), custom_call_target="tpu_custom_call" | custom-call | flops 1698693120 | bytes 4000000 | tf_op jit(solution)/shard_map/pallas_call | solution.py:235
  53.2 0.0 collective-permute-done.2.partial_ref
  53.2 0.8 %shard_map.49 = bf16[4,8,96,128]{3,2,1,0:T(8,128)(2,1)} custom-call(bf16[2,8,96,128]{3,2,1,0:T(8,128)(2,1)S(1)} %collective-permute-done.2.partial_ref, f32[2,8,96,128]{3,2,1,0:T(8,128)S(1)} %get-tuple-element.19.first_ref, bf16[4,8,96,128]{3,2,1,0:T(8,128)(2,1)} %get-tuple-element.20._), custom_call_target="tpu_custom_call", output_to_operand_aliasing={{}: (2, {})} | custom-call | flops 1000000 | bytes 2000000 | tf_op jit(solution)/shard_map/pallas_call | solution.py:246
  (1 shorter events, 0.0 us)
Async XLA Ops:
  0.0 11.9 %copy-start = (bf16[2,3,3,3,96,96]{5,4,3,2,1,0:T(8,128)(2,1)S(1)}, bf16[2,3,3,3,96,96]{5,4,3,2,1,0:T(8,128)(2,1)}, u32[]{:S(2)}) copy-start(bf16[2,3,3,3,96,96]{5,4,3,2,1,0:T(8,128)(2,1)} %param.6) | copy-start | bytes 2985988
  0.0 13.8 %copy-start.1 = (bf16[4,8,96,128]{3,2,1,0:T(8,128)(2,1)S(1)}, bf16[4,8,96,128]{3,2,1,0:T(8,128)(2,1)}, u32[]{:S(2)}) copy-start(bf16[4,8,96,128]{3,2,1,0:T(8,128)(2,1)} %stream_ref.3) | copy-start | bytes 2359300
  1.2 12.6 %collective-permute-start = (bf16[4,2,96,128]{3,2,1,0:T(8,128)(2,1)S(1)}, bf16[4,2,96,128]{3,2,1,0:T(8,128)(2,1)S(1)}, u32[]{:S(2)}, u32[]{:S(2)}) collective-permute-start(bf16[4,2,96,128]{3,2,1,0:T(8,128)(2,1)S(1)} %get-tuple-element.22), channel_id=1, source_target_pairs={{0,1},{1,2},{2,3},{4,5},{5,6},{6,7},{8,9},{9,10},{10,11},{12,13},{... | collective-permute-start | bytes 589832 | tf_op jit(solution)/shard_map/ppermute | solution.py:197
  5.8 8.0 %collective-permute-start.1 = (bf16[4,2,96,128]{3,2,1,0:T(8,128)(2,1)S(1)}, bf16[4,2,96,128]{3,2,1,0:T(8,128)(2,1)S(1)}, u32[]{:S(2)}, u32[]{:S(2)}) collective-permute-start(bf16[4,2,96,128]{3,2,1,0:T(8,128)(2,1)S(1)} %get-tuple-element.21), channel_id=1, source_target_pairs={{1,0},{2,1},{3,2},{5,4},{6,5},{7,6},{9,8},{10,9},{11,10},{13,12},{... | collective-permute-start | bytes 589832 | tf_op jit(solution)/shard_map/ppermute | solution.py:198
  8.7 12.5 %collective-permute-start.3 = (bf16[2,8,96,128]{3,2,1,0:T(8,128)(2,1)S(1)}, bf16[2,8,96,128]{3,2,1,0:T(8,128)(2,1)S(1)}, u32[]{:S(2)}, u32[]{:S(2)}) collective-permute-start(bf16[2,8,96,128]{3,2,1,0:T(8,128)(2,1)S(1)} %slice.17), channel_id=1, source_target_pairs={{0,4},{4,8},{8,12},{12,16},{16,20},{20,24},{24,28},{28,32},{32,36}... | collective-permute-start | bytes 1179656 | tf_op jit(solution)/shard_map/ppermute | solution.py:207
  12.0 0.7 %copy-start.2 = (f32[2,96]{1,0:T(2,128)S(1)}, f32[2,96]{1,0:T(2,128)}, u32[]{:S(2)}) copy-start(f32[2,96]{1,0:T(2,128)} %gains_ref.1) | copy-start | bytes 2308
  12.6 0.7 %copy-start.3 = (f32[2,96]{1,0:T(2,128)S(1)}, f32[2,96]{1,0:T(2,128)}, u32[]{:S(2)}) copy-start(f32[2,96]{1,0:T(2,128)} %biases_ref.1) | copy-start | bytes 2308
  18.0 35.2 %collective-permute-start.2 = (bf16[2,8,96,128]{3,2,1,0:T(8,128)(2,1)S(1)}, bf16[2,8,96,128]{3,2,1,0:T(8,128)(2,1)S(1)}, u32[]{:S(2)}, u32[]{:S(2)}) collective-permute-start(bf16[2,8,96,128]{3,2,1,0:T(8,128)(2,1)S(1)} %get-tuple-element.16), channel_id=1, source_target_pairs={{0,4},{4,8},{8,12},{12,16},{16,20},{20,24},{24,28},{28,32},{32,36}... | collective-permute-start | bytes 1179656 | tf_op jit(solution)/shard_map/ppermute | solution.py:233
  21.3 28.5 %collective-permute-start.4 = (bf16[2,2,96,128]{3,2,1,0:T(8,128)(2,1)S(1)}, bf16[2,2,96,128]{3,2,1,0:T(8,128)(2,1)S(1)}, u32[]{:S(2)}, u32[]{:S(2)}) collective-permute-start(bf16[2,2,96,128]{3,2,1,0:T(8,128)(2,1)S(1)} %get-tuple-element.24), channel_id=1, source_target_pairs={{0,1},{1,2},{2,3},{4,5},{5,6},{6,7},{8,9},{9,10},{10,11},{12,13},{... | collective-permute-start | bytes 294920 | tf_op jit(solution)/shard_map/ppermute | solution.py:197
  26.2 23.6 %collective-permute-start.5 = (bf16[2,2,96,128]{3,2,1,0:T(8,128)(2,1)S(1)}, bf16[2,2,96,128]{3,2,1,0:T(8,128)(2,1)S(1)}, u32[]{:S(2)}, u32[]{:S(2)}) collective-permute-start(bf16[2,2,96,128]{3,2,1,0:T(8,128)(2,1)S(1)} %get-tuple-element.23), channel_id=1, source_target_pairs={{1,0},{2,1},{3,2},{5,4},{6,5},{7,6},{9,8},{10,9},{11,10},{13,12},{... | collective-permute-start | bytes 294920 | tf_op jit(solution)/shard_map/ppermute | solution.py:198

commit v2 on v1

--- a/solution.py
+++ b/solution.py
@@ -214,7 +214,7 @@
             ((2, *plane), F32),
         ],
         flops=10**6,
-        moved=4 * 10**6,
+        moved=0,
     )(kernels.reshape(2, 3, 9 * channels, channels), gains, biases)
     sent, hidden, base = call(
         local_kernel,
@@ -227,8 +227,8 @@
             pltpu.VMEM((frames, rows + 4, 3 * channels, cols), BF16),
             pltpu.VMEM((2, rows + 2, 3 * channels, cols), BF16),
         ],
-        flops=mac * cells * 18,
-        moved=4 * 10**6,
+        flops=0,
+        moved=0,
     )(stream, above, below, weights, gain, bias)
     partial = lax.ppermute(sent, "tm", steps("tm", 1))
     above, below = row_edges(earlier)
@@ -239,8 +239,8 @@
             pltpu.VMEM((2, rows + 4, 3 * channels, cols), BF16),
             pltpu.VMEM((2, rows + 2, 3 * channels, cols), BF16),
         ],
-        flops=mac * cells * 10,
-        moved=4 * 10**6,
+        flops=0,
+        moved=0,
     )(earlier, above, below, hidden, base, stream, weights, gain, bias)
     block = pl.BlockSpec((2, rows, *plane), lambda i: (0, 0, 0, 0))
     return pl.pallas_call(

time: 54.3 us -> 66.8 us (1.23)
  the two profiles are of different devices: /device:TPU:135 before, /device:TPU:189 now
where the time goes in v2:
time: 66.8 us; the launch traced here: 66.5 us
  starting transfers between devices  46.8 us (70%)
  Pallas kernels  8.9 us (13%)
  waiting for transfers between devices  7.22 us (11%)
  local copies, waits for them, and re-layouts  3.49 us (5%)
    ppermute x1, starting transfers between devices, shards(): partial = lax.ppermute(sent, 'tm', steps('tm', 1))  31.4 us
    ppermute x2, starting transfers between devices, row_edges(): above = lax.ppermute(block[:, rows - 2:], 'rows', steps('rows', 1))  9.51 us
    ppermute x2, waiting for transfers between devices, row_edges(): below = lax.ppermute(block[:, :2], 'rows', steps('rows', -1))  7.21 us
    pallas_call x1, Pallas kernels, shards(): call(local_kernel, [((2, rows, *plane), BF16), ((2, rows + 2, *plane), F3...  4.23 us
    ppermute x2, starting transfers between devices, row_edges(): below = lax.ppermute(block[:, :2], 'rows', steps('rows', -1))  3.84 us
    pallas_call x1, Pallas kernels, shards(): call(history_kernel, [((frames, rows, *plane), BF16), ((2, rows, *plane),...  3.37 us
    ppermute x1, starting transfers between devices, shards(): earlier = lax.ppermute(stream[frames - 2:], 'tm', steps('tm', 1))  2.03 us
  transfers between devices with their start and end apart: 6, of which 2 were waited for; matrix products, arithmetic and copies ran while one was open for 2% of the time, Pallas kernels for 12%

profile of v2, /device:TPU:189, one launch (start us, length us, event | category | flops | bytes accessed | tf_op | source)
XLA Modules:
  0.0 66.5 jit_solution(872032918224137539)
XLA Ops:
  0.0 0.0 copy-start
  0.0 0.0 copy-start.2
  0.0 0.0 copy-start.3
  0.0 1.1 %slice.17 = bf16[2,8,96,128]{3,2,1,0:T(8,128)(2,1)S(1)} slice(bf16[4,8,96,128]{3,2,1,0:T(8,128)(2,1)} %stream_ref.3), slice={[2:4], [0:8], [0:96], [0:128]} | slice | bytes 786432 | tf_op jit(solution)/shard_map/slice | solution.py:207
  1.1 2.0 %collective-permute-start.3 = (bf16[2,8,96,128]{3,2,1,0:T(8,128)(2,1)S(1)}, bf16[2,8,96,128]{3,2,1,0:T(8,128)(2,1)S(1)}, u32[]{:S(2)}, u32[]{:S(2)}) collective-permute-start(bf16[2,8,96,128]{3,2,1,0:T(8,128)(2,1)S(1)} %slice.17), channel_id=1, source_target_pairs={{0,4},{4,8},{8,12},{12,16},{16,20},{20,24},{24,28},{28,32},{32,36}... | collective-permute-start | bytes 1179656 | tf_op jit(solution)/shard_map/ppermute | solution.py:207
  3.1 1.1 %fusion = (bf16[4,2,96,128]{3,2,1,0:T(8,128)(2,1)S(1)}, bf16[4,2,96,128]{3,2,1,0:T(8,128)(2,1)S(1)}) fusion(bf16[4,8,96,128]{3,2,1,0:T(8,128)(2,1)} %stream_ref.3), kind=kLoop, calls=%fused_computation | loop fusion | bytes 786432 | tf_op jit(solution)/shard_map/slice | solution.py:198
  4.2 4.8 %collective-permute-start = (bf16[4,2,96,128]{3,2,1,0:T(8,128)(2,1)S(1)}, bf16[4,2,96,128]{3,2,1,0:T(8,128)(2,1)S(1)}, u32[]{:S(2)}, u32[]{:S(2)}) collective-permute-start(bf16[4,2,96,128]{3,2,1,0:T(8,128)(2,1)S(1)} %get-tuple-element.22), channel_id=1, source_target_pairs={{0,1},{1,2},{2,3},{4,5},{5,6},{6,7},{8,9},{9,10},{10,11},{12,13},{... | collective-permute-start | bytes 589832 | tf_op jit(solution)/shard_map/ppermute | solution.py:197
  9.1 1.9 %collective-permute-start.1 = (bf16[4,2,96,128]{3,2,1,0:T(8,128)(2,1)S(1)}, bf16[4,2,96,128]{3,2,1,0:T(8,128)(2,1)S(1)}, u32[]{:S(2)}, u32[]{:S(2)}) collective-permute-start(bf16[4,2,96,128]{3,2,1,0:T(8,128)(2,1)S(1)} %get-tuple-element.21), channel_id=1, source_target_pairs={{1,0},{2,1},{3,2},{5,4},{6,5},{7,6},{9,8},{10,9},{11,10},{13,12},{... | collective-permute-start | bytes 589832 | tf_op jit(solution)/shard_map/ppermute | solution.py:198
  11.0 0.0 copy-done.2
  11.0 0.0 copy-done.3
  11.0 0.0 copy-start.1
  11.0 1.3 %copy-done.1 = bf16[2,3,3,3,96,96]{5,4,3,2,1,0:T(8,128)(2,1)S(1)} copy-done((bf16[2,3,3,3,96,96]{5,4,3,2,1,0:T(8,128)(2,1)S(1)}, bf16[2,3,3,3,96,96]{5,4,3,2,1,0:T(8,128)(2,1)}, u32[]{:S(2)}) %copy-start.1) | copy-done | bytes 995352
  12.3 0.5 shard_map.46
  12.8 0.0 collective-permute-done.above_ref
  12.8 3.2 %collective-permute-done.1.below_ref = bf16[4,2,96,128]{3,2,1,0:T(8,128)(2,1)S(1)} collective-permute-done((bf16[4,2,96,128]{3,2,1,0:T(8,128)(2,1)S(1)}, bf16[4,2,96,128]{3,2,1,0:T(8,128)(2,1)S(1)}, u32[]{:S(2)}, u32[]{:S(2)}) %collective-permute-start.1) | collective-permute-done | bytes 196640 | tf_op jit(solution)/shard_map/ppermute | solution.py:198
  16.0 0.0 copy-done
  16.0 4.2 %shard_map.47 = (bf16[2,8,96,128]{3,2,1,0:T(8,128)(2,1)S(1)}, f32[2,10,96,128]{3,2,1,0:T(8,128)S(1)}, f32[2,8,96,128]{3,2,1,0:T(8,128)S(1)}) custom-call(bf16[4,8,96,128]{3,2,1,0:T(8,128)(2,1)S(1)} %copy-done, bf16[4,2,96,128]{3,2,1,0:T(8,128)(2,1)S(1)} %collective-permute-done.above_ref, bf16[4,2,96,128]{3,2,1,0:T(8,128)(2,1)S(1)} %collective-permute-done.1.below_ref, ...), custom_call_target="tpu_custom_call" | custom-call | tf_op jit(solution)/shard_map/pallas_call | solution.py:219
  20.3 31.4 %collective-permute-start.2 = (bf16[2,8,96,128]{3,2,1,0:T(8,128)(2,1)S(1)}, bf16[2,8,96,128]{3,2,1,0:T(8,128)(2,1)S(1)}, u32[]{:S(2)}, u32[]{:S(2)}) collective-permute-start(bf16[2,8,96,128]{3,2,1,0:T(8,128)(2,1)S(1)} %get-tuple-element.16), channel_id=1, source_target_pairs={{0,4},{4,8},{8,12},{12,16},{16,20},{20,24},{24,28},{28,32},{32,36}... | collective-permute-start | bytes 1179656 | tf_op jit(solution)/shard_map/ppermute | solution.py:233
  51.7 0.0 collective-permute-done.3.earlier_ref
  51.7 4.7 %collective-permute-start.4 = (bf16[2,2,96,128]{3,2,1,0:T(8,128)(2,1)S(1)}, bf16[2,2,96,128]{3,2,1,0:T(8,128)(2,1)S(1)}, u32[]{:S(2)}, u32[]{:S(2)}) collective-permute-start(bf16[2,2,96,128]{3,2,1,0:T(8,128)(2,1)S(1)} %get-tuple-element.24), channel_id=1, source_target_pairs={{0,1},{1,2},{2,3},{4,5},{5,6},{6,7},{8,9},{9,10},{10,11},{12,13},{... | collective-permute-start | bytes 294920 | tf_op jit(solution)/shard_map/ppermute | solution.py:197
  56.4 1.9 %collective-permute-start.5 = (bf16[2,2,96,128]{3,2,1,0:T(8,128)(2,1)S(1)}, bf16[2,2,96,128]{3,2,1,0:T(8,128)(2,1)S(1)}, u32[]{:S(2)}, u32[]{:S(2)}) collective-permute-start(bf16[2,2,96,128]{3,2,1,0:T(8,128)(2,1)S(1)} %get-tuple-element.23), channel_id=1, source_target_pairs={{1,0},{2,1},{3,2},{5,4},{6,5},{7,6},{9,8},{10,9},{11,10},{13,12},{... | collective-permute-start | bytes 294920 | tf_op jit(solution)/shard_map/ppermute | solution.py:198
  58.3 0.0 collective-permute-done.4.above_ref
  58.3 4.0 %collective-permute-done.5.below_ref = bf16[2,2,96,128]{3,2,1,0:T(8,128)(2,1)S(1)} collective-permute-done((bf16[2,2,96,128]{3,2,1,0:T(8,128)(2,1)S(1)}, bf16[2,2,96,128]{3,2,1,0:T(8,128)(2,1)S(1)}, u32[]{:S(2)}, u32[]{:S(2)}) %collective-permute-start.5) | collective-permute-done | bytes 98336 | tf_op jit(solution)/shard_map/ppermute | solution.py:198
  62.3 3.4 %shard_map.48 = (bf16[4,8,96,128]{3,2,1,0:T(8,128)(2,1)}, f32[2,8,96,128]{3,2,1,0:T(8,128)S(1)}) custom-call(bf16[2,8,96,128]{3,2,1,0:T(8,128)(2,1)S(1)} %collective-permute-done.3.earlier_ref, bf16[2,2,96,128]{3,2,1,0:T(8,128)(2,1)S(1)} %collective-permute-done.4.above_ref, bf16[2,2,96,128]{3,2,1,0:T(8,128)(2,1)S(1)} %collective-permute-done.5.below_ref, ...), custom_call_target="tpu_custom_call" | custom-call | tf_op jit(solution)/shard_map/pallas_call | solution.py:235
  65.7 0.0 collective-permute-done.2.partial_ref
  65.7 0.8 %shard_map.49 = bf16[4,8,96,128]{3,2,1,0:T(8,128)(2,1)} custom-call(bf16[2,8,96,128]{3,2,1,0:T(8,128)(2,1)S(1)} %collective-permute-done.2.partial_ref, f32[2,8,96,128]{3,2,1,0:T(8,128)S(1)} %get-tuple-element.19.first_ref, bf16[4,8,96,128]{3,2,1,0:T(8,128)(2,1)} %get-tuple-element.20._), custom_call_target="tpu_custom_call", output_to_operand_aliasing={{}: (2, {})} | custom-call | flops 1000000 | bytes 2000000 | tf_op jit(solution)/shard_map/pallas_call | solution.py:246
  (1 shorter events, 0.0 us)
Async XLA Ops:
  0.0 16.0 %copy-start = (bf16[4,8,96,128]{3,2,1,0:T(8,128)(2,1)S(1)}, bf16[4,8,96,128]{3,2,1,0:T(8,128)(2,1)}, u32[]{:S(2)}) copy-start(bf16[4,8,96,128]{3,2,1,0:T(8,128)(2,1)} %stream_ref.3) | copy-start | bytes 2359300
  0.0 11.0 %copy-start.2 = (f32[2,96]{1,0:T(2,128)S(1)}, f32[2,96]{1,0:T(2,128)}, u32[]{:S(2)}) copy-start(f32[2,96]{1,0:T(2,128)} %gains_ref.1) | copy-start | bytes 2308
  0.0 11.0 %copy-start.3 = (f32[2,96]{1,0:T(2,128)S(1)}, f32[2,96]{1,0:T(2,128)}, u32[]{:S(2)}) copy-start(f32[2,96]{1,0:T(2,128)} %biases_ref.1) | copy-start | bytes 2308
  1.1 50.6 %collective-permute-start.3 = (bf16[2,8,96,128]{3,2,1,0:T(8,128)(2,1)S(1)}, bf16[2,8,96,128]{3,2,1,0:T(8,128)(2,1)S(1)}, u32[]{:S(2)}, u32[]{:S(2)}) collective-permute-start(bf16[2,8,96,128]{3,2,1,0:T(8,128)(2,1)S(1)} %slice.17), channel_id=1, source_target_pairs={{0,4},{4,8},{8,12},{12,16},{16,20},{20,24},{24,28},{28,32},{32,36}... | collective-permute-start | bytes 1179656 | tf_op jit(solution)/shard_map/ppermute | solution.py:207
  4.2 8.6 %collective-permute-start = (bf16[4,2,96,128]{3,2,1,0:T(8,128)(2,1)S(1)}, bf16[4,2,96,128]{3,2,1,0:T(8,128)(2,1)S(1)}, u32[]{:S(2)}, u32[]{:S(2)}) collective-permute-start(bf16[4,2,96,128]{3,2,1,0:T(8,128)(2,1)S(1)} %get-tuple-element.22), channel_id=1, source_target_pairs={{0,1},{1,2},{2,3},{4,5},{5,6},{6,7},{8,9},{9,10},{10,11},{12,13},{... | collective-permute-start | bytes 589832 | tf_op jit(solution)/shard_map/ppermute | solution.py:197
  9.1 7.0 %collective-permute-start.1 = (bf16[4,2,96,128]{3,2,1,0:T(8,128)(2,1)S(1)}, bf16[4,2,96,128]{3,2,1,0:T(8,128)(2,1)S(1)}, u32[]{:S(2)}, u32[]{:S(2)}) collective-permute-start(bf16[4,2,96,128]{3,2,1,0:T(8,128)(2,1)S(1)} %get-tuple-element.21), channel_id=1, source_target_pairs={{1,0},{2,1},{3,2},{5,4},{6,5},{7,6},{9,8},{10,9},{11,10},{13,12},{... | collective-permute-start | bytes 589832 | tf_op jit(solution)/shard_map/ppermute | solution.py:198
  11.0 1.3 %copy-start.1 = (bf16[2,3,3,3,96,96]{5,4,3,2,1,0:T(8,128)(2,1)S(1)}, bf16[2,3,3,3,96,96]{5,4,3,2,1,0:T(8,128)(2,1)}, u32[]{:S(2)}) copy-start(bf16[2,3,3,3,96,96]{5,4,3,2,1,0:T(8,128)(2,1)} %param.6) | copy-start | bytes 2985988
  20.3 45.4 %collective-permute-start.2 = (bf16[2,8,96,128]{3,2,1,0:T(8,128)(2,1)S(1)}, bf16[2,8,96,128]{3,2,1,0:T(8,128)(2,1)S(1)}, u32[]{:S(2)}, u32[]{:S(2)}) collective-permute-start(bf16[2,8,96,128]{3,2,1,0:T(8,128)(2,1)S(1)} %get-tuple-element.16), channel_id=1, source_target_pairs={{0,4},{4,8},{8,12},{12,16},{16,20},{20,24},{24,28},{28,32},{32,36}... | collective-permute-start | bytes 1179656 | tf_op jit(solution)/shard_map/ppermute | solution.py:233
  51.7 6.6 %collective-permute-start.4 = (bf16[2,2,96,128]{3,2,1,0:T(8,128)(2,1)S(1)}, bf16[2,2,96,128]{3,2,1,0:T(8,128)(2,1)S(1)}, u32[]{:S(2)}, u32[]{:S(2)}) collective-permute-start(bf16[2,2,96,128]{3,2,1,0:T(8,128)(2,1)S(1)} %get-tuple-element.24), channel_id=1, source_target_pairs={{0,1},{1,2},{2,3},{4,5},{5,6},{6,7},{8,9},{9,10},{10,11},{12,13},{... | collective-permute-start | bytes 294920 | tf_op jit(solution)/shard_map/ppermute | solution.py:197
  56.4 5.9 %collective-permute-start.5 = (bf16[2,2,96,128]{3,2,1,0:T(8,128)(2,1)S(1)}, bf16[2,2,96,128]{3,2,1,0:T(8,128)(2,1)S(1)}, u32[]{:S(2)}, u32[]{:S(2)}) collective-permute-start(bf16[2,2,96,128]{3,2,1,0:T(8,128)(2,1)S(1)} %get-tuple-element.23), channel_id=1, source_target_pairs={{1,0},{2,1},{3,2},{5,4},{6,5},{7,6},{9,8},{10,9},{11,10},{13,12},{... | collective-permute-start | bytes 294920 | tf_op jit(solution)/shard_map/ppermute | solution.py:198

commit v3 on v2

--- a/solution.py
+++ b/solution.py
@@ -8,7 +8,7 @@
 from jax.sharding import PartitionSpec as P
 
 EPS = 1e-06
-VMEM_BYTES = 48 * 1024 * 1024
+VMEM_BYTES = 20 * 1024 * 1024
 F32 = jnp.float32
 BF16 = jnp.bfloat16
 
@@ -66,8 +66,48 @@
     return pair[:, :cols], pair[:, cols:]
 
 
+def activate_rows(taps_ref, frames, odd, own, partner_ref, across, gain):
+    rows = taps_ref.shape[1] - 4
+    for frame in range(frames):
+        for row in range(rows + 4):
+            if row < 2:
+                values = jnp.where(odd, partner_ref[frame, row], across(frame, row, 0))
+            elif row < rows + 2:
+                values = own(frame, row - 2)
+            else:
+                edge = row - rows - 2
+                values = jnp.where(odd, across(frame, edge, rows), partner_ref[frame, edge])
+            store_taps(taps_ref, frame, row, activated(values.astype(F32), gain))
+
+
+def widen_kernel(stream_ref, across_ref, out_ref):
+    frames, rows = stream_ref.shape[:2]
+    odd = lax.axis_index("rows") % 2 == 1
+    for frame in range(2):
+        source = frames - 2 + frame
+        out_ref[frame, pl.ds(jnp.where(odd, 0, 2), rows)] = stream_ref[source]
+        out_ref[frame, pl.ds(jnp.where(odd, rows, 0), 2)] = across_ref[source]
+
+
+def halo_source():
+    band = lax.axis_index("rows")
+    outer_band = (band == 0) | (band == lax.axis_size("rows") - 1)
+    first_block = lax.axis_index("tm") % span("tm") == 0
+    return outer_band, outer_band & first_block
+
+
+def edge_kernel(outer_ref, relayed_ref, inner_ref, out_ref):
+    rows = outer_ref.shape[1]
+    outer_band, relay = halo_source()
+    odd = lax.axis_index("rows") % 2 == 1
+    near = pl.ds(jnp.where(odd, 0, rows - 2), 2)
+    wide = pl.ds(jnp.where(odd, 0, rows), 2)
+    direct = jnp.where(outer_band, outer_ref[:, near], inner_ref[:, wide])
+    out_ref[...] = jnp.where(relay, relayed_ref[:, near], direct)
+
+
 def local_kernel(
-    stream_ref, above_ref, below_ref, weights_ref, gain_ref, bias_ref,
+    stream_ref, partner_ref, across_ref, weights_ref, gain_ref, bias_ref,
     send_ref, hidden_ref, base_ref,
     taps_ref, normed_ref,
 ):
@@ -75,16 +115,18 @@
     band = lax.axis_index("rows")
     keep_above = jnp.where(band > 0, 1.0, 0.0)
     keep_below = jnp.where(band < lax.axis_size("rows") - 1, 1.0, 0.0)
+    odd = band % 2 == 1
     gain = gain_ref[0]
-    for frame in range(frames):
-        for row in range(rows + 4):
-            if row < 2:
-                values = above_ref[frame, row]
-            elif row < rows + 2:
-                values = stream_ref[frame, row - 2]
-            else:
-                values = below_ref[frame, row - rows - 2]
-            store_taps(taps_ref, frame, row, activated(values.astype(F32), gain))
+
+    activate_rows(
+        taps_ref,
+        frames,
+        odd,
+        lambda frame, row: stream_ref[frame, row],
+        partner_ref,
+        lambda frame, row, _: across_ref[frame, row],
+        gain,
+    )
     gain = gain_ref[1]
     bias = jnp.concatenate([bias_ref[0]] * 2, axis=1)
     for pair in range((rows + 2) // 2):
@@ -125,24 +167,33 @@
 
 
 def history_kernel(
-    earlier_ref, above_ref, below_ref, hidden_ref, base_ref, stream_ref, weights_ref, gain_ref, bias_ref,
+    outer_ref, relayed_ref, inner_ref, partner_ref, hidden_ref, base_ref, stream_ref, weights_ref, gain_ref, bias_ref,
     out_ref, first_ref,
     taps_ref, normed_ref,
 ):
-    rows = earlier_ref.shape[1]
+    rows = outer_ref.shape[1]
     band = lax.axis_index("rows")
     keep_above = jnp.where(band > 0, 1.0, 0.0)
     keep_below = jnp.where(band < lax.axis_size("rows") - 1, 1.0, 0.0)
+    odd = band % 2 == 1
     gain = gain_ref[0]
-    for frame in range(2):
-        for row in range(rows + 4):
-            if row < 2:
-                values = above_ref[frame, row]
-            elif row < rows + 2:
-                values = earlier_ref[frame, row - 2]
-            else:
-                values = below_ref[frame, row - rows - 2]
-            store_taps(taps_ref, frame, row, activated(values.astype(F32), gain))
+
+    outer_band, relay = halo_source()
+    shift = jnp.where(odd, 0, 2)
+
+    def own(frame, row):
+        direct = jnp.where(outer_band, outer_ref[frame, row], inner_ref[frame, row + shift])
+        return jnp.where(relay, relayed_ref[frame, row], direct)
+
+    activate_rows(
+        taps_ref,
+        2,
+        odd,
+        own,
+        partner_ref,
+        lambda frame, row, start: inner_ref[frame, row + start],
+        gain,
+    )
     gain = gain_ref[1]
     for pair in range((rows + 2) // 2):
         y0 = tap_products(weights_ref, 0, (0, 0), row_pair(taps_ref, 0, 2 * pair))
@@ -187,16 +238,27 @@
     )
 
 
+def span(axis):
+    return lax.axis_size(axis) // 4
+
+
 def steps(axis, distance):
     size = lax.axis_size(axis)
     return [(i, i + distance) for i in range(size) if 0 <= i + distance < size]
 
 
-def row_edges(block):
-    rows = block.shape[1]
-    above = lax.ppermute(block[:, rows - 2 :], "rows", steps("rows", 1))
-    below = lax.ppermute(block[:, :2], "rows", steps("rows", -1))
-    return above, below
+def spread(pairs, bands):
+    size = lax.axis_size("rows")
+    return [(i * size + source, j * size + target) for i, j in pairs for source, target in bands]
+
+
+def band_part(block, late):
+    start = jnp.where(late, block.shape[1] - 2, 0)
+    return lax.dynamic_slice_in_dim(block, start, 2, axis=1)
+
+
+def partners(block):
+    return lax.ppermute(block, "rows", [(0, 1), (1, 0), (2, 3), (3, 2)])
 
 
 def shards(stream, gains, kernels, biases):
@@ -204,8 +266,18 @@
     plane = (channels, cols)
     cells = rows * cols
     mac = 2 * 9 * channels * channels
-    earlier = lax.ppermute(stream[frames - 2 :], "tm", steps("tm", 1))
-    above, below = row_edges(stream)
+    odd = lax.axis_index("rows") % 2 == 1
+    following = steps("tm", 1)
+    across = lax.ppermute(band_part(stream, odd), "rows", [(1, 2), (2, 1)])
+    mesh_axes = ("tm", "rows")
+    outer_bands, inner_bands = [(0, 0), (3, 3)], [(1, 1), (2, 2)]
+    size, group = lax.axis_size("tm"), span("tm")
+    detour = [(i, i + 1 if (i + 1) % group else i + 1 - group) for i in range(size - 1)]
+    onward = [(i, i + group) for i in range(0, size - group, group)]
+    outer = lax.ppermute(stream[frames - 2 :], mesh_axes, spread(detour, outer_bands))
+    partner = partners(band_part(stream, ~odd))
+    (widened,) = call(widen_kernel, [((2, rows + 2, *plane), BF16)])(stream, across)
+    inner = lax.ppermute(widened, mesh_axes, spread(following, inner_bands))
     weights, gain, bias = call(
         prepare_kernel,
         [
@@ -229,9 +301,12 @@
         ],
         flops=0,
         moved=0,
-    )(stream, above, below, weights, gain, bias)
-    partial = lax.ppermute(sent, "tm", steps("tm", 1))
-    above, below = row_edges(earlier)
+    )(stream, partner, across, weights, gain, bias)
+    sent, outer = lax.optimization_barrier((sent, outer))
+    partial = lax.ppermute(sent, "tm", following)
+    relayed = lax.ppermute(outer, mesh_axes, spread(onward, outer_bands))
+    (edge,) = call(edge_kernel, [((2, 2, *plane), BF16)])(outer, relayed, inner)
+    beside = partners(edge)
     out, first = call(
         history_kernel,
         [((frames, rows, *plane), BF16), ((2, rows, *plane), F32)],
@@ -241,7 +316,7 @@
         ],
         flops=0,
         moved=0,
-    )(earlier, above, below, hidden, base, stream, weights, gain, bias)
+    )(outer, relayed, inner, beside, hidden, base, stream, weights, gain, bias)
     block = pl.BlockSpec((2, rows, *plane), lambda i: (0, 0, 0, 0))
     return pl.pallas_call(
         finish_kernel,

time: 66.8 us -> 49.8 us (0.75)
  the two profiles are of different devices: /device:TPU:189 before, /device:TPU:256 now
where the time goes in v3:
time: 49.8 us; the launch traced here: 49.5 us
  waiting for transfers between devices  21.1 us (42%)
  starting transfers between devices  17 us (34%)
  Pallas kernels  9.05 us (18%)
  local copies, waits for them, and re-layouts  2.18 us (4%)
    ppermute x1, waiting for transfers between devices, shards(): partial = lax.ppermute(sent, 'tm', following)  10.8 us
    ppermute x1, waiting for transfers between devices, shards(): relayed = lax.ppermute(outer, mesh_axes, spread(onward, outer_bands))  8.84 us
    ppermute x2, starting transfers between devices, partners(): return lax.ppermute(block, 'rows', [(0, 1), (1, 0), (2, 3), (3, 2)])  6.24 us
    pallas_call x1, Pallas kernels, shards(): call(local_kernel, [((2, rows, *plane), BF16), ((2, rows + 2, *plane), F3...  4.22 us
    ppermute x1, starting transfers between devices, shards(): relayed = lax.ppermute(outer, mesh_axes, spread(onward, outer_bands))  3.82 us
    ppermute x1, starting transfers between devices, shards(): lax.ppermute(stream[frames - 2:], mesh_axes, spread(detour, outer_bands))  3.62 us
    pallas_call x1, Pallas kernels, shards(): call(history_kernel, [((frames, rows, *plane), BF16), ((2, rows, *plane),...  3.44 us
    ppermute x1, starting transfers between devices, shards(): partial = lax.ppermute(sent, 'tm', following)  1.92 us
  transfers between devices with their start and end apart: 7, of which 5 were waited for; matrix products, arithmetic and copies ran while one was open for 2% of the time, Pallas kernels for 17%

profile of v3, /device:TPU:256, one launch (start us, length us, event | category | flops | bytes accessed | tf_op | source)
XLA Modules:
  0.0 49.5 jit_solution(247089085689755472)
XLA Ops:
  0.0 0.0 copy-start
  0.0 1.1 %slice.3 = bf16[2,8,96,128]{3,2,1,0:T(8,128)(2,1)S(1)} slice(bf16[4,8,96,128]{3,2,1,0:T(8,128)(2,1)} %stream_ref.5), slice={[2:4], [0:8], [0:96], [0:128]} | slice | bytes 786432 | tf_op jit(solution)/shard_map/slice | solution.py:277
  1.1 0.0 copy-start.1
  1.1 0.0 copy-start.2
  1.1 0.0 copy-start.3
  1.1 3.6 %collective-permute-start.2 = (bf16[2,8,96,128]{3,2,1,0:T(8,128)(2,1)S(1)}, bf16[2,8,96,128]{3,2,1,0:T(8,128)(2,1)S(1)}, u32[]{:S(2)}, u32[]{:S(2)}) collective-permute-start(bf16[2,8,96,128]{3,2,1,0:T(8,128)(2,1)S(1)} %slice.3), channel_id=1, source_target_pairs={{0,4},{3,7},{4,8},{7,11},{8,12},{11,15},{12,16},{15,19},{16,20},{1... | collective-permute-start | bytes 1179656 | tf_op jit(solution)/shard_map/ppermute | solution.py:277
  4.8 1.1 %constant_dynamic-slice_fusion = (bf16[4,2,96,128]{3,2,1,0:T(8,128)(2,1)S(1)}, bf16[4,2,96,128]{3,2,1,0:T(8,128)(2,1)S(1)}) fusion(bf16[4,8,96,128]{3,2,1,0:T(8,128)(2,1)} %stream_ref.5, s32[]{:T(128)S(6)} %select_n.18, s32[]{:T(128)S(6)} %select_n.17), kind=kLoop, calls=%fused_computation | loop fusion | bytes 786440 | tf_op jit(solution)/shard_map/dynamic_slice | solution.py:257
  5.8 0.7 %collective-permute-start.1 = (bf16[4,2,96,128]{3,2,1,0:T(8,128)(2,1)S(1)}, bf16[4,2,96,128]{3,2,1,0:T(8,128)(2,1)S(1)}, u32[]{:S(2)}, u32[]{:S(2)}) collective-permute-start(bf16[4,2,96,128]{3,2,1,0:T(8,128)(2,1)S(1)} %get-tuple-element.25), channel_id=1, source_target_pairs={{1,2},{2,1},{5,6},{6,5},{9,10},{10,9},{13,14},{14,13},{17,18},{18,... | collective-permute-start | bytes 589832 | tf_op jit(solution)/shard_map/ppermute | solution.py:271
  6.5 1.9 %collective-permute-start = (bf16[4,2,96,128]{3,2,1,0:T(8,128)(2,1)S(1)}, bf16[4,2,96,128]{3,2,1,0:T(8,128)(2,1)S(1)}, u32[]{:S(2)}, u32[]{:S(2)}) collective-permute-start(bf16[4,2,96,128]{3,2,1,0:T(8,128)(2,1)S(1)} %get-tuple-element.26), channel_id=1, source_target_pairs={{0,1},{1,0},{2,3},{3,2},{4,5},{5,4},{6,7},{7,6},{8,9},{9,8},{10,11... | collective-permute-start | bytes 589832 | tf_op jit(solution)/shard_map/ppermute | solution.py:261
  8.5 0.0 collective-permute-done.1.across_ref
  8.5 0.0 copy-done
  8.5 0.1 shard_map.48
  8.5 0.7 %collective-permute-start.5 = (bf16[2,10,96,128]{3,2,1,0:T(8,128)(2,1)S(1)}, bf16[2,10,96,128]{3,2,1,0:T(8,128)(2,1)S(1)}, u32[]{:S(2)}, u32[]{:S(2)}) collective-permute-start(bf16[2,10,96,128]{3,2,1,0:T(8,128)(2,1)S(1)} %shard_map.48), channel_id=1, source_target_pairs={{1,5},{2,6},{5,9},{6,10},{9,13},{10,14},{13,17},{14,18},{17,21},{1... | collective-permute-start | bytes 1474568 | tf_op jit(solution)/shard_map/ppermute | solution.py:280
  9.2 0.0 copy-done.1
  9.3 0.0 copy-done.2
  9.3 0.0 copy-done.3
  9.3 0.5 shard_map.46
  9.8 0.1 collective-permute-done.partner_ref
  9.9 4.2 %shard_map.47 = (bf16[2,8,96,128]{3,2,1,0:T(8,128)(2,1)S(1)}, f32[2,10,96,128]{3,2,1,0:T(8,128)S(1)}, f32[2,8,96,128]{3,2,1,0:T(8,128)S(1)}) custom-call(bf16[4,8,96,128]{3,2,1,0:T(8,128)(2,1)S(1)} %copy-done, bf16[4,2,96,128]{3,2,1,0:T(8,128)(2,1)S(1)} %collective-permute-done.partner_ref, bf16[4,2,96,128]{3,2,1,0:T(8,128)(2,1)S(1)} %collective-permute-done.1.across_ref, ...), custom_call_target="tpu_custom_call" | custom-call | tf_op jit(solution)/shard_map/pallas_call | solution.py:291
  14.1 0.5 %collective-permute-done.2.outer_ref = bf16[2,8,96,128]{3,2,1,0:T(8,128)(2,1)S(1)} collective-permute-done((bf16[2,8,96,128]{3,2,1,0:T(8,128)(2,1)S(1)}, bf16[2,8,96,128]{3,2,1,0:T(8,128)(2,1)S(1)}, u32[]{:S(2)}, u32[]{:S(2)}) %collective-permute-start.2) | collective-permute-done | bytes 393248 | tf_op jit(solution)/shard_map/ppermute | solution.py:277
  14.6 3.8 %collective-permute-start.4 = (bf16[2,8,96,128]{3,2,1,0:T(8,128)(2,1)S(1)}, bf16[2,8,96,128]{3,2,1,0:T(8,128)(2,1)S(1)}, u32[]{:S(2)}, u32[]{:S(2)}) collective-permute-start(bf16[2,8,96,128]{3,2,1,0:T(8,128)(2,1)S(1)} %collective-permute-done.2.outer_ref), channel_id=1, source_target_pairs={{0,128},{3,131},{128,256},{131,259},{256,384},{259,387}} | collective-permute-start | bytes 1179656 | tf_op jit(solution)/shard_map/ppermute | solution.py:307
  18.4 1.9 %collective-permute-start.3 = (bf16[2,8,96,128]{3,2,1,0:T(8,128)(2,1)S(1)}, bf16[2,8,96,128]{3,2,1,0:T(8,128)(2,1)S(1)}, u32[]{:S(2)}, u32[]{:S(2)}) collective-permute-start(bf16[2,8,96,128]{3,2,1,0:T(8,128)(2,1)S(1)} %get-tuple-element.19), channel_id=1, source_target_pairs={{0,4},{4,8},{8,12},{12,16},{16,20},{20,24},{24,28},{28,32},{32,36}... | collective-permute-start | bytes 1179656 | tf_op jit(solution)/shard_map/ppermute | solution.py:306
  20.3 0.0 collective-permute-done.5.inner_ref
  20.4 8.8 %collective-permute-done.4.relayed_ref = bf16[2,8,96,128]{3,2,1,0:T(8,128)(2,1)S(1)} collective-permute-done((bf16[2,8,96,128]{3,2,1,0:T(8,128)(2,1)S(1)}, bf16[2,8,96,128]{3,2,1,0:T(8,128)(2,1)S(1)}, u32[]{:S(2)}, u32[]{:S(2)}) %collective-permute-start.4) | collective-permute-done | bytes 393248 | tf_op jit(solution)/shard_map/ppermute | solution.py:307
  29.2 4.3 %collective-permute-start.6 = (bf16[2,2,96,128]{3,2,1,0:T(8,128)(2,1)S(1)}, bf16[2,2,96,128]{3,2,1,0:T(8,128)(2,1)S(1)}, u32[]{:S(2)}, u32[]{:S(2)}) collective-permute-start(bf16[2,2,96,128]{3,2,1,0:T(8,128)(2,1)S(1)} %shard_map.49), channel_id=1, source_target_pairs={{0,1},{1,0},{2,3},{3,2},{4,5},{5,4},{6,7},{7,6},{8,9},{9,8},{10,11... | collective-permute-start | bytes 294920 | tf_op jit(solution)/shard_map/ppermute | solution.py:261
  33.6 0.9 %collective-permute-done.6.partner_ref = bf16[2,2,96,128]{3,2,1,0:T(8,128)(2,1)S(1)} collective-permute-done((bf16[2,2,96,128]{3,2,1,0:T(8,128)(2,1)S(1)}, bf16[2,2,96,128]{3,2,1,0:T(8,128)(2,1)S(1)}, u32[]{:S(2)}, u32[]{:S(2)}) %collective-permute-start.6) | collective-permute-done | bytes 98336 | tf_op jit(solution)/shard_map/ppermute | solution.py:261
  34.5 3.4 %shard_map.50 = (bf16[4,8,96,128]{3,2,1,0:T(8,128)(2,1)}, f32[2,8,96,128]{3,2,1,0:T(8,128)S(1)}) custom-call(bf16[2,8,96,128]{3,2,1,0:T(8,128)(2,1)S(1)} %collective-permute-done.2.outer_ref, bf16[2,8,96,128]{3,2,1,0:T(8,128)(2,1)S(1)} %collective-permute-done.4.relayed_ref, bf16[2,10,96,128]{3,2,1,0:T(8,128)(2,1)S(1)} %collective-permute-done.5.inner_ref, ...), custom_call_target="tpu_custom_call" | custom-call | tf_op jit(solution)/shard_map/pallas_call | solution.py:310
  37.9 10.8 %collective-permute-done.3.partial_ref = bf16[2,8,96,128]{3,2,1,0:T(8,128)(2,1)S(1)} collective-permute-done((bf16[2,8,96,128]{3,2,1,0:T(8,128)(2,1)S(1)}, bf16[2,8,96,128]{3,2,1,0:T(8,128)(2,1)S(1)}, u32[]{:S(2)}, u32[]{:S(2)}) %collective-permute-start.3) | collective-permute-done | bytes 393248 | tf_op jit(solution)/shard_map/ppermute | solution.py:306
  48.7 0.8 %shard_map.51 = bf16[4,8,96,128]{3,2,1,0:T(8,128)(2,1)} custom-call(bf16[2,8,96,128]{3,2,1,0:T(8,128)(2,1)S(1)} %collective-permute-done.3.partial_ref, f32[2,8,96,128]{3,2,1,0:T(8,128)S(1)} %get-tuple-element.23.first_ref, bf16[4,8,96,128]{3,2,1,0:T(8,128)(2,1)} %get-tuple-element.24._), custom_call_target="tpu_custom_call", output_to_operand_aliasing={{}: (2, {})} | custom-call | flops 1000000 | bytes 2000000 | tf_op jit(solution)/shard_map/pallas_call | solution.py:321
  (1 shorter events, 0.0 us)
Async XLA Ops:
  0.0 8.5 %copy-start = (bf16[4,8,96,128]{3,2,1,0:T(8,128)(2,1)S(1)}, bf16[4,8,96,128]{3,2,1,0:T(8,128)(2,1)}, u32[]{:S(2)}) copy-start(bf16[4,8,96,128]{3,2,1,0:T(8,128)(2,1)} %stream_ref.5) | copy-start | bytes 2359300
  1.1 8.1 %copy-start.1 = (bf16[2,3,3,3,96,96]{5,4,3,2,1,0:T(8,128)(2,1)S(1)}, bf16[2,3,3,3,96,96]{5,4,3,2,1,0:T(8,128)(2,1)}, u32[]{:S(2)}) copy-start(bf16[2,3,3,3,96,96]{5,4,3,2,1,0:T(8,128)(2,1)} %param.6) | copy-start | bytes 2985988
  1.1 8.1 %copy-start.2 = (f32[2,96]{1,0:T(2,128)S(1)}, f32[2,96]{1,0:T(2,128)}, u32[]{:S(2)}) copy-start(f32[2,96]{1,0:T(2,128)} %gains_ref.1) | copy-start | bytes 2308
  1.1 8.1 %copy-start.3 = (f32[2,96]{1,0:T(2,128)S(1)}, f32[2,96]{1,0:T(2,128)}, u32[]{:S(2)}) copy-start(f32[2,96]{1,0:T(2,128)} %biases_ref.1) | copy-start | bytes 2308
  1.1 13.5 %collective-permute-start.2 = (bf16[2,8,96,128]{3,2,1,0:T(8,128)(2,1)S(1)}, bf16[2,8,96,128]{3,2,1,0:T(8,128)(2,1)S(1)}, u32[]{:S(2)}, u32[]{:S(2)}) collective-permute-start(bf16[2,8,96,128]{3,2,1,0:T(8,128)(2,1)S(1)} %slice.3), channel_id=1, source_target_pairs={{0,4},{3,7},{4,8},{7,11},{8,12},{11,15},{12,16},{15,19},{16,20},{1... | collective-permute-start | bytes 1179656 | tf_op jit(solution)/shard_map/ppermute | solution.py:277
  5.8 2.6 %collective-permute-start.1 = (bf16[4,2,96,128]{3,2,1,0:T(8,128)(2,1)S(1)}, bf16[4,2,96,128]{3,2,1,0:T(8,128)(2,1)S(1)}, u32[]{:S(2)}, u32[]{:S(2)}) collective-permute-start(bf16[4,2,96,128]{3,2,1,0:T(8,128)(2,1)S(1)} %get-tuple-element.25), channel_id=1, source_target_pairs={{1,2},{2,1},{5,6},{6,5},{9,10},{10,9},{13,14},{14,13},{17,18},{18,... | collective-permute-start | bytes 589832 | tf_op jit(solution)/shard_map/ppermute | solution.py:271
  6.5 3.3 %collective-permute-start = (bf16[4,2,96,128]{3,2,1,0:T(8,128)(2,1)S(1)}, bf16[4,2,96,128]{3,2,1,0:T(8,128)(2,1)S(1)}, u32[]{:S(2)}, u32[]{:S(2)}) collective-permute-start(bf16[4,2,96,128]{3,2,1,0:T(8,128)(2,1)S(1)} %get-tuple-element.26), channel_id=1, source_target_pairs={{0,1},{1,0},{2,3},{3,2},{4,5},{5,4},{6,7},{7,6},{8,9},{9,8},{10,11... | collective-permute-start | bytes 589832 | tf_op jit(solution)/shard_map/ppermute | solution.py:261
  8.5 11.8 %collective-permute-start.5 = (bf16[2,10,96,128]{3,2,1,0:T(8,128)(2,1)S(1)}, bf16[2,10,96,128]{3,2,1,0:T(8,128)(2,1)S(1)}, u32[]{:S(2)}, u32[]{:S(2)}) collective-permute-start(bf16[2,10,96,128]{3,2,1,0:T(8,128)(2,1)S(1)} %shard_map.48), channel_id=1, source_target_pairs={{1,5},{2,6},{5,9},{6,10},{9,13},{10,14},{13,17},{14,18},{17,21},{1... | collective-permute-start | bytes 1474568 | tf_op jit(solution)/shard_map/ppermute | solution.py:280
  14.6 14.6 %collective-permute-start.4 = (bf16[2,8,96,128]{3,2,1,0:T(8,128)(2,1)S(1)}, bf16[2,8,96,128]{3,2,1,0:T(8,128)(2,1)S(1)}, u32[]{:S(2)}, u32[]{:S(2)}) collective-permute-start(bf16[2,8,96,128]{3,2,1,0:T(8,128)(2,1)S(1)} %collective-permute-done.2.outer_ref), channel_id=1, source_target_pairs={{0,128},{3,131},{128,256},{131,259},{256,384},{259,387}} | collective-permute-start | bytes 1179656 | tf_op jit(solution)/shard_map/ppermute | solution.py:307
  18.4 30.3 %collective-permute-start.3 = (bf16[2,8,96,128]{3,2,1,0:T(8,128)(2,1)S(1)}, bf16[2,8,96,128]{3,2,1,0:T(8,128)(2,1)S(1)}, u32[]{:S(2)}, u32[]{:S(2)}) collective-permute-start(bf16[2,8,96,128]{3,2,1,0:T(8,128)(2,1)S(1)} %get-tuple-element.19), channel_id=1, source_target_pairs={{0,4},{4,8},{8,12},{12,16},{16,20},{20,24},{24,28},{28,32},{32,36}... | collective-permute-start | bytes 1179656 | tf_op jit(solution)/shard_map/ppermute | solution.py:306
  29.2 5.2 %collective-permute-start.6 = (bf16[2,2,96,128]{3,2,1,0:T(8,128)(2,1)S(1)}, bf16[2,2,96,128]{3,2,1,0:T(8,128)(2,1)S(1)}, u32[]{:S(2)}, u32[]{:S(2)}) collective-permute-start(bf16[2,2,96,128]{3,2,1,0:T(8,128)(2,1)S(1)} %shard_map.49), channel_id=1, source_target_pairs={{0,1},{1,0},{2,3},{3,2},{4,5},{5,4},{6,7},{7,6},{8,9},{9,8},{10,11... | collective-permute-start | bytes 294920 | tf_op jit(solution)/shard_map/ppermute | solution.py:261

commit v4 on v3

--- a/solution.py
+++ b/solution.py
@@ -80,30 +80,26 @@
             store_taps(taps_ref, frame, row, activated(values.astype(F32), gain))
 
 
-def widen_kernel(stream_ref, across_ref, out_ref):
-    frames, rows = stream_ref.shape[:2]
-    odd = lax.axis_index("rows") % 2 == 1
-    for frame in range(2):
-        source = frames - 2 + frame
-        out_ref[frame, pl.ds(jnp.where(odd, 0, 2), rows)] = stream_ref[source]
-        out_ref[frame, pl.ds(jnp.where(odd, rows, 0), 2)] = across_ref[source]
-
-
-def halo_source():
+def first_block_bands():
     band = lax.axis_index("rows")
     outer_band = (band == 0) | (band == lax.axis_size("rows") - 1)
     first_block = lax.axis_index("tm") % span("tm") == 0
-    return outer_band, outer_band & first_block
-
-
-def edge_kernel(outer_ref, relayed_ref, inner_ref, out_ref):
-    rows = outer_ref.shape[1]
-    outer_band, relay = halo_source()
+    return first_block & outer_band, first_block & jnp.logical_not(outer_band)
+
+
+def narrow_kernel(earlier_ref, out_ref):
+    half = out_ref.shape[1]
+    start = jnp.where(lax.axis_index("rows") == 1, half, 0)
+    out_ref[...] = earlier_ref[:, pl.ds(start, half)]
+
+
+def edge_kernel(earlier_ref, narrow_ref, rest_ref, out_ref):
+    relay, _ = first_block_bands()
+    rows = earlier_ref.shape[1]
     odd = lax.axis_index("rows") % 2 == 1
     near = pl.ds(jnp.where(odd, 0, rows - 2), 2)
-    wide = pl.ds(jnp.where(odd, 0, rows), 2)
-    direct = jnp.where(outer_band, outer_ref[:, near], inner_ref[:, wide])
-    out_ref[...] = jnp.where(relay, relayed_ref[:, near], direct)
+    relayed = jnp.where(odd, narrow_ref[:, :2], rest_ref[:, rows // 2 - 2 :])
+    out_ref[...] = jnp.where(relay, relayed, earlier_ref[:, near])
 
 
 def local_kernel(
@@ -167,23 +163,27 @@
 
 
 def history_kernel(
-    outer_ref, relayed_ref, inner_ref, partner_ref, hidden_ref, base_ref, stream_ref, weights_ref, gain_ref, bias_ref,
+    earlier_ref, narrow_ref, rest_ref, corner_ref, partner_ref, hidden_ref, base_ref, stream_ref, weights_ref, gain_ref, bias_ref,
     out_ref, first_ref,
     taps_ref, normed_ref,
 ):
-    rows = outer_ref.shape[1]
+    rows = earlier_ref.shape[1]
     band = lax.axis_index("rows")
     keep_above = jnp.where(band > 0, 1.0, 0.0)
     keep_below = jnp.where(band < lax.axis_size("rows") - 1, 1.0, 0.0)
     odd = band % 2 == 1
     gain = gain_ref[0]
 
-    outer_band, relay = halo_source()
-    shift = jnp.where(odd, 0, 2)
+    relay, swap = first_block_bands()
 
     def own(frame, row):
-        direct = jnp.where(outer_band, outer_ref[frame, row], inner_ref[frame, row + shift])
-        return jnp.where(relay, relayed_ref[frame, row], direct)
+        half = rows // 2
+        relayed = narrow_ref[frame, row] if row < half else rest_ref[frame, row - half]
+        return jnp.where(relay, relayed, earlier_ref[frame, row])
+
+    def across(frame, row, start):
+        swapped = narrow_ref[frame, row + (rows // 2 - 2 if start == 0 else 0)]
+        return jnp.where(swap, swapped, corner_ref[frame, row])
 
     activate_rows(
         taps_ref,
@@ -191,7 +191,7 @@
         odd,
         own,
         partner_ref,
-        lambda frame, row, start: inner_ref[frame, row + start],
+        across,
         gain,
     )
     gain = gain_ref[1]
@@ -272,12 +272,19 @@
     mesh_axes = ("tm", "rows")
     outer_bands, inner_bands = [(0, 0), (3, 3)], [(1, 1), (2, 2)]
     size, group = lax.axis_size("tm"), span("tm")
-    detour = [(i, i + 1 if (i + 1) % group else i + 1 - group) for i in range(size - 1)]
     onward = [(i, i + group) for i in range(0, size - group, group)]
-    outer = lax.ppermute(stream[frames - 2 :], mesh_axes, spread(detour, outer_bands))
+    crossing = [(i, j) for i, j in following if j % group == 0]
+    straight = [(i, j) for i, j in following if j % group]
+    turned = [(i, j - group) for i, j in crossing]
+    first_blocks = [(j, j) for _, j in crossing]
+    earlier = lax.ppermute(
+        stream[frames - 2 :],
+        mesh_axes,
+        spread(straight, outer_bands + inner_bands)
+        + spread(turned, outer_bands)
+        + spread(crossing, inner_bands),
+    )
     partner = partners(band_part(stream, ~odd))
-    (widened,) = call(widen_kernel, [((2, rows + 2, *plane), BF16)])(stream, across)
-    inner = lax.ppermute(widened, mesh_axes, spread(following, inner_bands))
     weights, gain, bias = call(
         prepare_kernel,
         [
@@ -302,10 +309,17 @@
         flops=0,
         moved=0,
     )(stream, partner, across, weights, gain, bias)
-    sent, outer = lax.optimization_barrier((sent, outer))
+    corner, sent = lax.optimization_barrier((across[frames - 2 :], sent))
     partial = lax.ppermute(sent, "tm", following)
-    relayed = lax.ppermute(outer, mesh_axes, spread(onward, outer_bands))
-    (edge,) = call(edge_kernel, [((2, 2, *plane), BF16)])(outer, relayed, inner)
+    corner = lax.ppermute(corner, mesh_axes, spread(straight, inner_bands))
+    earlier, corner = lax.optimization_barrier((earlier, corner))
+    half = rows // 2
+    (narrow,) = call(narrow_kernel, [((2, half, *plane), BF16)])(earlier)
+    narrow = lax.ppermute(
+        narrow, mesh_axes, spread(onward, outer_bands) + spread(first_blocks, [(1, 2), (2, 1)])
+    )
+    rest = lax.ppermute(earlier[:, half:], mesh_axes, spread(onward, outer_bands))
+    (edge,) = call(edge_kernel, [((2, 2, *plane), BF16)])(earlier, narrow, rest)
     beside = partners(edge)
     out, first = call(
         history_kernel,
@@ -316,7 +330,7 @@
         ],
         flops=0,
         moved=0,
-    )(outer, relayed, inner, beside, hidden, base, stream, weights, gain, bias)
+    )(earlier, narrow, rest, corner, beside, hidden, base, stream, weights, gain, bias)
     block = pl.BlockSpec((2, rows, *plane), lambda i: (0, 0, 0, 0))
     return pl.pallas_call(
         finish_kernel,

time: 49.8 us -> 46.3 us (0.930)
  the two profiles are of different devices: /device:TPU:256 before, /device:TPU:1 now
where the time goes in v4:
time: 46.3 us; the launch traced here: 46 us
  starting transfers between devices  33.1 us (71%)
  Pallas kernels  9.03 us (20%)
  local copies, waits for them, and re-layouts  2.23 us (5%)
  waiting for transfers between devices  1.45 us (3%)
    ppermute x2, starting transfers between devices, partners(): return lax.ppermute(block, 'rows', [(0, 1), (1, 0), (2, 3), (3, 2)])  16.2 us
    ppermute x1, starting transfers between devices, shards(): across = lax.ppermute(band_part(stream, odd), 'rows', [(1, 2), (2, 1)])  4.84 us
    pallas_call x1, Pallas kernels, shards(): call(local_kernel, [((2, rows, *plane), BF16), ((2, rows + 2, *plane), F3...  4.23 us
    ppermute x1, starting transfers between devices, shards(): lax.ppermute(stream[frames - 2:], mesh_axes, spread(straight, outer_bands...  4.19 us
    pallas_call x1, Pallas kernels, shards(): call(history_kernel, [((frames, rows, *plane), BF16), ((2, rows, *plane),...  3.44 us
    ppermute x1, starting transfers between devices, shards(): corner = lax.ppermute(corner, mesh_axes, spread(straight, inner_bands))  3.32 us
    ppermute x1, starting transfers between devices, shards(): partial = lax.ppermute(sent, 'tm', following)  3.22 us
    slice x1, local copies, waits for them, and re-layouts, shards(): stream[frames - 2:]  1.13 us
  transfers between devices with their start and end apart: 8, of which 3 were waited for; matrix products, arithmetic and copies ran while one was open for 2% of the time, Pallas kernels for 18%

profile of v4, /device:TPU:1, one launch (start us, length us, event | category | flops | bytes accessed | tf_op | source)
XLA Modules:
  0.0 46.0 jit_solution(7657361527084654394)
XLA Ops:
  0.0 0.0 copy-start.3
  0.0 0.0 copy-start.1
  0.0 0.0 copy-start.2
  0.0 1.1 %slice.10 = bf16[2,8,96,128]{3,2,1,0:T(8,128)(2,1)S(1)} slice(bf16[4,8,96,128]{3,2,1,0:T(8,128)(2,1)} %stream_ref.3), slice={[2:4], [0:8], [0:96], [0:128]} | slice | bytes 786432 | tf_op jit(solution)/shard_map/slice | solution.py:281
  1.1 0.0 copy-start
  1.2 4.2 %collective-permute-start.3 = (bf16[2,8,96,128]{3,2,1,0:T(8,128)(2,1)S(1)}, bf16[2,8,96,128]{3,2,1,0:T(8,128)(2,1)S(1)}, u32[]{:S(2)}, u32[]{:S(2)}) collective-permute-start(bf16[2,8,96,128]{3,2,1,0:T(8,128)(2,1)S(1)} %slice.10), channel_id=1, source_target_pairs={{0,4},{3,7},{1,5},{2,6},{4,8},{7,11},{5,9},{6,10},{8,12},{11,15},{... | collective-permute-start | bytes 1179656 | tf_op jit(solution)/shard_map/ppermute | solution.py:280
  5.4 1.1 %constant_dynamic-slice_fusion = (bf16[4,2,96,128]{3,2,1,0:T(8,128)(2,1)S(1)}, bf16[4,2,96,128]{3,2,1,0:T(8,128)(2,1)S(1)}) fusion(bf16[4,8,96,128]{3,2,1,0:T(8,128)(2,1)} %stream_ref.3, s32[]{:T(128)S(6)} %select_n.18, s32[]{:T(128)S(6)} %select_n.17), kind=kLoop, calls=%fused_computation | loop fusion | bytes 786440 | tf_op jit(solution)/shard_map/dynamic_slice | solution.py:257
  6.4 4.8 %collective-permute-start = (bf16[4,2,96,128]{3,2,1,0:T(8,128)(2,1)S(1)}, bf16[4,2,96,128]{3,2,1,0:T(8,128)(2,1)S(1)}, u32[]{:S(2)}, u32[]{:S(2)}) collective-permute-start(bf16[4,2,96,128]{3,2,1,0:T(8,128)(2,1)S(1)} %get-tuple-element.30), channel_id=1, source_target_pairs={{1,2},{2,1},{5,6},{6,5},{9,10},{10,9},{13,14},{14,13},{17,18},{18,... | collective-permute-start | bytes 589832 | tf_op jit(solution)/shard_map/ppermute | solution.py:271
  11.3 2.5 %collective-permute-start.1 = (bf16[4,2,96,128]{3,2,1,0:T(8,128)(2,1)S(1)}, bf16[4,2,96,128]{3,2,1,0:T(8,128)(2,1)S(1)}, u32[]{:S(2)}, u32[]{:S(2)}) collective-permute-start(bf16[4,2,96,128]{3,2,1,0:T(8,128)(2,1)S(1)} %get-tuple-element.29), channel_id=1, source_target_pairs={{0,1},{1,0},{2,3},{3,2},{4,5},{5,4},{6,7},{7,6},{8,9},{9,8},{10,11... | collective-permute-start | bytes 589832 | tf_op jit(solution)/shard_map/ppermute | solution.py:261
  13.8 0.0 copy-done.3
  13.8 0.0 copy-done.1
  13.8 0.0 copy-done.2
  13.8 0.5 %shard_map.46 = (bf16[2,288,864]{2,1,0:T(8,128)(2,1)S(1)}, f32[2,96,128]{2,1,0:T(8,128)S(1)}, f32[2,96,128]{2,1,0:T(8,128)S(1)}) custom-call(bf16[2,3,864,96]{3,2,1,0:T(8,128)(2,1)S(1)} %bitcast.1, f32[2,96]{1,0:T(2,128)S(1)} %copy-done.2, f32[2,96]{1,0:T(2,128)S(1)} %copy-done.3), custom_call_target="tpu_custom_call" | custom-call | flops 1000000 | tf_op jit(solution)/shard_map/pallas_call | solution.py:288
  14.3 0.3 collective-permute-done.across_ref
  14.6 0.2 collective-permute-done.1.partner_ref
  14.8 0.0 copy-done
  14.8 4.2 %shard_map.47 = (bf16[2,8,96,128]{3,2,1,0:T(8,128)(2,1)S(1)}, f32[2,10,96,128]{3,2,1,0:T(8,128)S(1)}, f32[2,8,96,128]{3,2,1,0:T(8,128)S(1)}) custom-call(bf16[4,8,96,128]{3,2,1,0:T(8,128)(2,1)S(1)} %copy-done, bf16[4,2,96,128]{3,2,1,0:T(8,128)(2,1)S(1)} %collective-permute-done.1.partner_ref, bf16[4,2,96,128]{3,2,1,0:T(8,128)(2,1)S(1)} %collective-permute-done.across_ref, ...), custom_call_target="tpu_custom_call" | custom-call | tf_op jit(solution)/shard_map/pallas_call | solution.py:298
  19.0 3.3 %collective-permute-start.4 = (bf16[2,2,96,128]{3,2,1,0:T(8,128)(2,1)S(1)}, bf16[2,2,96,128]{3,2,1,0:T(8,128)(2,1)S(1)}, u32[]{:S(2)}, u32[]{:S(2)}) collective-permute-start(bf16[2,2,96,128]{3,2,1,0:T(8,128)(2,1)S(1)} %slice.12), channel_id=1, source_target_pairs={{1,5},{2,6},{5,9},{6,10},{9,13},{10,14},{13,17},{14,18},{17,21},{1... | collective-permute-start | bytes 294920 | tf_op jit(solution)/shard_map/ppermute | solution.py:314
  22.4 3.2 %collective-permute-start.2 = (bf16[2,8,96,128]{3,2,1,0:T(8,128)(2,1)S(1)}, bf16[2,8,96,128]{3,2,1,0:T(8,128)(2,1)S(1)}, u32[]{:S(2)}, u32[]{:S(2)}) collective-permute-start(bf16[2,8,96,128]{3,2,1,0:T(8,128)(2,1)S(1)} %get-tuple-element.21), channel_id=1, source_target_pairs={{0,4},{4,8},{8,12},{12,16},{16,20},{20,24},{24,28},{28,32},{32,36}... | collective-permute-start | bytes 1179656 | tf_op jit(solution)/shard_map/ppermute | solution.py:313
  25.6 0.0 collective-permute-done.4.corner_ref
  25.6 0.0 collective-permute-done.3.earlier_ref
  25.7 0.7 %collective-permute-start.5 = (bf16[2,4,96,128]{3,2,1,0:T(8,128)(2,1)S(1)}, bf16[2,4,96,128]{3,2,1,0:T(8,128)(2,1)S(1)}, u32[]{:S(2)}, u32[]{:S(2)}) collective-permute-start(bf16[2,4,96,128]{3,2,1,0:T(8,128)(2,1)S(1)} %shard_map.48), channel_id=1, source_target_pairs={{0,128},{3,131},{128,256},{131,259},{256,384},{259,387},{129,130},... | collective-permute-start | bytes 589832 | tf_op jit(solution)/shard_map/ppermute | solution.py:318
  26.4 0.7 %collective-permute-start.6 = (bf16[2,4,96,128]{3,2,1,0:T(8,128)(2,1)S(1)}, bf16[2,4,96,128]{3,2,1,0:T(8,128)(2,1)S(1)}, u32[]{:S(2)}, u32[]{:S(2)}) collective-permute-start(bf16[2,4,96,128]{3,2,1,0:T(8,128)(2,1)S(1)} %slice.11), channel_id=1, source_target_pairs={{0,128},{3,131},{128,256},{131,259},{256,384},{259,387}} | collective-permute-start | bytes 589832 | tf_op jit(solution)/shard_map/ppermute | solution.py:321
  27.0 0.0 collective-permute-done.5.narrow_ref
  27.1 0.0 collective-permute-done.6.rest_ref
  27.1 13.7 %collective-permute-start.7 = (bf16[2,2,96,128]{3,2,1,0:T(8,128)(2,1)S(1)}, bf16[2,2,96,128]{3,2,1,0:T(8,128)(2,1)S(1)}, u32[]{:S(2)}, u32[]{:S(2)}) collective-permute-start(bf16[2,2,96,128]{3,2,1,0:T(8,128)(2,1)S(1)} %shard_map.49), channel_id=1, source_target_pairs={{0,1},{1,0},{2,3},{3,2},{4,5},{5,4},{6,7},{7,6},{8,9},{9,8},{10,11... | collective-permute-start | bytes 294920 | tf_op jit(solution)/shard_map/ppermute | solution.py:261
  40.8 0.9 %collective-permute-done.7.partner_ref = bf16[2,2,96,128]{3,2,1,0:T(8,128)(2,1)S(1)} collective-permute-done((bf16[2,2,96,128]{3,2,1,0:T(8,128)(2,1)S(1)}, bf16[2,2,96,128]{3,2,1,0:T(8,128)(2,1)S(1)}, u32[]{:S(2)}, u32[]{:S(2)}) %collective-permute-start.7) | collective-permute-done | bytes 98336 | tf_op jit(solution)/shard_map/ppermute | solution.py:261
  41.8 3.4 %shard_map.50 = (bf16[4,8,96,128]{3,2,1,0:T(8,128)(2,1)}, f32[2,8,96,128]{3,2,1,0:T(8,128)S(1)}) custom-call(bf16[2,8,96,128]{3,2,1,0:T(8,128)(2,1)S(1)} %collective-permute-done.3.earlier_ref, bf16[2,4,96,128]{3,2,1,0:T(8,128)(2,1)S(1)} %collective-permute-done.5.narrow_ref, bf16[2,4,96,128]{3,2,1,0:T(8,128)(2,1)S(1)} %collective-permute-done.6.rest_ref, ...), custom_call_target="tpu_custom_call" | custom-call | tf_op jit(solution)/shard_map/pallas_call | solution.py:324
  45.2 0.0 collective-permute-done.2.partial_ref
  45.2 0.8 %shard_map.51 = bf16[4,8,96,128]{3,2,1,0:T(8,128)(2,1)} custom-call(bf16[2,8,96,128]{3,2,1,0:T(8,128)(2,1)S(1)} %collective-permute-done.2.partial_ref, f32[2,8,96,128]{3,2,1,0:T(8,128)S(1)} %get-tuple-element.27.first_ref, bf16[4,8,96,128]{3,2,1,0:T(8,128)(2,1)} %get-tuple-element.28._), custom_call_target="tpu_custom_call", output_to_operand_aliasing={{}: (2, {})} | custom-call | flops 1000000 | bytes 2000000 | tf_op jit(solution)/shard_map/pallas_call | solution.py:335
  (4 shorter events, 0.1 us)
Async XLA Ops:
  0.0 13.8 %copy-start.3 = (f32[2,96]{1,0:T(2,128)S(1)}, f32[2,96]{1,0:T(2,128)}, u32[]{:S(2)}) copy-start(f32[2,96]{1,0:T(2,128)} %biases_ref.1) | copy-start | bytes 2308
  0.0 13.8 %copy-start.1 = (bf16[2,3,3,3,96,96]{5,4,3,2,1,0:T(8,128)(2,1)S(1)}, bf16[2,3,3,3,96,96]{5,4,3,2,1,0:T(8,128)(2,1)}, u32[]{:S(2)}) copy-start(bf16[2,3,3,3,96,96]{5,4,3,2,1,0:T(8,128)(2,1)} %param.6) | copy-start | bytes 2985988
  0.0 13.8 %copy-start.2 = (f32[2,96]{1,0:T(2,128)S(1)}, f32[2,96]{1,0:T(2,128)}, u32[]{:S(2)}) copy-start(f32[2,96]{1,0:T(2,128)} %gains_ref.1) | copy-start | bytes 2308
  1.1 13.7 %copy-start = (bf16[4,8,96,128]{3,2,1,0:T(8,128)(2,1)S(1)}, bf16[4,8,96,128]{3,2,1,0:T(8,128)(2,1)}, u32[]{:S(2)}) copy-start(bf16[4,8,96,128]{3,2,1,0:T(8,128)(2,1)} %stream_ref.3) | copy-start | bytes 2359300
  1.2 24.5 %collective-permute-start.3 = (bf16[2,8,96,128]{3,2,1,0:T(8,128)(2,1)S(1)}, bf16[2,8,96,128]{3,2,1,0:T(8,128)(2,1)S(1)}, u32[]{:S(2)}, u32[]{:S(2)}) collective-permute-start(bf16[2,8,96,128]{3,2,1,0:T(8,128)(2,1)S(1)} %slice.10), channel_id=1, source_target_pairs={{0,4},{3,7},{1,5},{2,6},{4,8},{7,11},{5,9},{6,10},{8,12},{11,15},{... | collective-permute-start | bytes 1179656 | tf_op jit(solution)/shard_map/ppermute | solution.py:280
  6.4 8.2 %collective-permute-start = (bf16[4,2,96,128]{3,2,1,0:T(8,128)(2,1)S(1)}, bf16[4,2,96,128]{3,2,1,0:T(8,128)(2,1)S(1)}, u32[]{:S(2)}, u32[]{:S(2)}) collective-permute-start(bf16[4,2,96,128]{3,2,1,0:T(8,128)(2,1)S(1)} %get-tuple-element.30), channel_id=1, source_target_pairs={{1,2},{2,1},{5,6},{6,5},{9,10},{10,9},{13,14},{14,13},{17,18},{18,... | collective-permute-start | bytes 589832 | tf_op jit(solution)/shard_map/ppermute | solution.py:271
  11.3 3.5 %collective-permute-start.1 = (bf16[4,2,96,128]{3,2,1,0:T(8,128)(2,1)S(1)}, bf16[4,2,96,128]{3,2,1,0:T(8,128)(2,1)S(1)}, u32[]{:S(2)}, u32[]{:S(2)}) collective-permute-start(bf16[4,2,96,128]{3,2,1,0:T(8,128)(2,1)S(1)} %get-tuple-element.29), channel_id=1, source_target_pairs={{0,1},{1,0},{2,3},{3,2},{4,5},{5,4},{6,7},{7,6},{8,9},{9,8},{10,11... | collective-permute-start | bytes 589832 | tf_op jit(solution)/shard_map/ppermute | solution.py:261
  19.0 6.6 %collective-permute-start.4 = (bf16[2,2,96,128]{3,2,1,0:T(8,128)(2,1)S(1)}, bf16[2,2,96,128]{3,2,1,0:T(8,128)(2,1)S(1)}, u32[]{:S(2)}, u32[]{:S(2)}) collective-permute-start(bf16[2,2,96,128]{3,2,1,0:T(8,128)(2,1)S(1)} %slice.12), channel_id=1, source_target_pairs={{1,5},{2,6},{5,9},{6,10},{9,13},{10,14},{13,17},{14,18},{17,21},{1... | collective-permute-start | bytes 294920 | tf_op jit(solution)/shard_map/ppermute | solution.py:314
  22.4 22.8 %collective-permute-start.2 = (bf16[2,8,96,128]{3,2,1,0:T(8,128)(2,1)S(1)}, bf16[2,8,96,128]{3,2,1,0:T(8,128)(2,1)S(1)}, u32[]{:S(2)}, u32[]{:S(2)}) collective-permute-start(bf16[2,8,96,128]{3,2,1,0:T(8,128)(2,1)S(1)} %get-tuple-element.21), channel_id=1, source_target_pairs={{0,4},{4,8},{8,12},{12,16},{16,20},{20,24},{24,28},{28,32},{32,36}... | collective-permute-start | bytes 1179656 | tf_op jit(solution)/shard_map/ppermute | solution.py:313
  25.7 1.4 %collective-permute-start.5 = (bf16[2,4,96,128]{3,2,1,0:T(8,128)(2,1)S(1)}, bf16[2,4,96,128]{3,2,1,0:T(8,128)(2,1)S(1)}, u32[]{:S(2)}, u32[]{:S(2)}) collective-permute-start(bf16[2,4,96,128]{3,2,1,0:T(8,128)(2,1)S(1)} %shard_map.48), channel_id=1, source_target_pairs={{0,128},{3,131},{128,256},{131,259},{256,384},{259,387},{129,130},... | collective-permute-start | bytes 589832 | tf_op jit(solution)/shard_map/ppermute | solution.py:318
  26.4 0.7 %collective-permute-start.6 = (bf16[2,4,96,128]{3,2,1,0:T(8,128)(2,1)S(1)}, bf16[2,4,96,128]{3,2,1,0:T(8,128)(2,1)S(1)}, u32[]{:S(2)}, u32[]{:S(2)}) collective-permute-start(bf16[2,4,96,128]{3,2,1,0:T(8,128)(2,1)S(1)} %slice.11), channel_id=1, source_target_pairs={{0,128},{3,131},{128,256},{131,259},{256,384},{259,387}} | collective-permute-start | bytes 589832 | tf_op jit(solution)/shard_map/ppermute | solution.py:321
  27.1 14.6 %collective-permute-start.7 = (bf16[2,2,96,128]{3,2,1,0:T(8,128)(2,1)S(1)}, bf16[2,2,96,128]{3,2,1,0:T(8,128)(2,1)S(1)}, u32[]{:S(2)}, u32[]{:S(2)}) collective-permute-start(bf16[2,2,96,128]{3,2,1,0:T(8,128)(2,1)S(1)} %shard_map.49), channel_id=1, source_target_pairs={{0,1},{1,0},{2,3},{3,2},{4,5},{5,4},{6,7},{7,6},{8,9},{9,8},{10,11... | collective-permute-start | bytes 294920 | tf_op jit(solution)/shard_map/ppermute | solution.py:261

commit v5 on v4

--- a/solution.py
+++ b/solution.py
@@ -50,7 +50,36 @@
     }
 
 
-def prepare_kernel(kernels_ref, gains_ref, biases_ref, weights_ref, gain_ref, bias_ref):
+def cut_kernel(stream_ref, recent_ref, across_ref, partner_ref, sems):
+    frames, rows = stream_ref.shape[:2]
+    odd = lax.axis_index("rows") % 2 == 1
+    outward = pl.ds(jnp.where(odd, rows - 2, 0), 2)
+    inward = pl.ds(jnp.where(odd, 0, rows - 2), 2)
+    copies = [
+        pltpu.make_async_copy(stream_ref.at[pl.ds(frames - 2, 2)], recent_ref, sems.at[0]),
+        pltpu.make_async_copy(stream_ref.at[:, outward], across_ref, sems.at[1]),
+        pltpu.make_async_copy(stream_ref.at[:, inward], partner_ref, sems.at[2]),
+    ]
+    for copy in copies:
+        copy.start()
+    for copy in copies:
+        copy.wait()
+
+
+def prepare_kernel(
+    all_kernels_ref, all_gains_ref, all_biases_ref,
+    weights_ref, gain_ref, bias_ref,
+    kernels_ref, gains_ref, biases_ref, sems,
+):
+    copies = [
+        pltpu.make_async_copy(all_kernels_ref, kernels_ref, sems.at[0]),
+        pltpu.make_async_copy(all_gains_ref, gains_ref, sems.at[1]),
+        pltpu.make_async_copy(all_biases_ref, biases_ref, sems.at[2]),
+    ]
+    for copy in copies:
+        copy.start()
+    for copy in copies:
+        copy.wait()
     channels = gains_ref.shape[1]
     cols = gain_ref.shape[2]
     for index in range(2):
@@ -252,11 +281,6 @@
     return [(i * size + source, j * size + target) for i, j in pairs for source, target in bands]
 
 
-def band_part(block, late):
-    start = jnp.where(late, block.shape[1] - 2, 0)
-    return lax.dynamic_slice_in_dim(block, start, 2, axis=1)
-
-
 def partners(block):
     return lax.ppermute(block, "rows", [(0, 1), (1, 0), (2, 3), (3, 2)])
 
@@ -266,9 +290,16 @@
     plane = (channels, cols)
     cells = rows * cols
     mac = 2 * 9 * channels * channels
-    odd = lax.axis_index("rows") % 2 == 1
+    edges = jax.ShapeDtypeStruct((frames, 2, *plane), BF16)
+    recent, upper, lower = pl.pallas_call(
+        cut_kernel,
+        out_shape=[jax.ShapeDtypeStruct((2, rows, *plane), BF16), edges, edges],
+        in_specs=[pl.BlockSpec(memory_space=pltpu.HBM)],
+        scratch_shapes=[pltpu.SemaphoreType.DMA((3,))],
+        compiler_params=pltpu.CompilerParams(vmem_limit_bytes=4 * 1024 * 1024),
+    )(stream)
     following = steps("tm", 1)
-    across = lax.ppermute(band_part(stream, odd), "rows", [(1, 2), (2, 1)])
+    across = lax.ppermute(upper, "rows", [(1, 2), (2, 1)])
     mesh_axes = ("tm", "rows")
     outer_bands, inner_bands = [(0, 0), (3, 3)], [(1, 1), (2, 2)]
     size, group = lax.axis_size("tm"), span("tm")
@@ -278,23 +309,31 @@
     turned = [(i, j - group) for i, j in crossing]
     first_blocks = [(j, j) for _, j in crossing]
     earlier = lax.ppermute(
-        stream[frames - 2 :],
+        recent,
         mesh_axes,
         spread(straight, outer_bands + inner_bands)
         + spread(turned, outer_bands)
         + spread(crossing, inner_bands),
     )
-    partner = partners(band_part(stream, ~odd))
-    weights, gain, bias = call(
+    partner = partners(lower)
+    taps = kernels.reshape(2, 3, 9 * channels, channels)
+    weights, gain, bias = pl.pallas_call(
         prepare_kernel,
-        [
-            ((2, 3 * channels, 9 * channels), BF16),
-            ((2, *plane), F32),
-            ((2, *plane), F32),
-        ],
-        flops=10**6,
-        moved=0,
-    )(kernels.reshape(2, 3, 9 * channels, channels), gains, biases)
+        out_shape=[
+            jax.ShapeDtypeStruct((2, 3 * channels, 9 * channels), BF16),
+            jax.ShapeDtypeStruct((2, *plane), F32),
+            jax.ShapeDtypeStruct((2, *plane), F32),
+        ],
+        in_specs=[pl.BlockSpec(memory_space=pltpu.HBM)] * 3,
+        scratch_shapes=[
+            pltpu.VMEM(taps.shape, BF16),
+            pltpu.VMEM(gains.shape, F32),
+            pltpu.VMEM(biases.shape, F32),
+            pltpu.SemaphoreType.DMA((3,)),
+        ],
+        compiler_params=pltpu.CompilerParams(vmem_limit_bytes=VMEM_BYTES),
+        cost_estimate=pl.CostEstimate(flops=10**6, bytes_accessed=0, transcendentals=0),
+    )(taps, gains, biases)
     sent, hidden, base = call(
         local_kernel,
         [
@@ -309,10 +348,10 @@
         flops=0,
         moved=0,
     )(stream, partner, across, weights, gain, bias)
+    partial = lax.ppermute(sent, "tm", following)
     corner, sent = lax.optimization_barrier((across[frames - 2 :], sent))
-    partial = lax.ppermute(sent, "tm", following)
     corner = lax.ppermute(corner, mesh_axes, spread(straight, inner_bands))
-    earlier, corner = lax.optimization_barrier((earlier, corner))
+    earlier, sent = lax.optimization_barrier((earlier, sent))
     half = rows // 2
     (narrow,) = call(narrow_kernel, [((2, half, *plane), BF16)])(earlier)
     narrow = lax.ppermute(

time: 46.3 us -> 44.9 us (0.970)
  the two profiles are of different devices: /device:TPU:1 before, /device:TPU:129 now
where the time goes in v5:
time: 44.9 us; the launch traced here: 44.5 us
  starting transfers between devices  24.1 us (54%)
  Pallas kernels  9.51 us (21%)
  waiting for transfers between devices  6.91 us (15%)
  local copies, waits for them, and re-layouts  3.83 us (9%)
    ppermute x2, starting transfers between devices, partners(): return lax.ppermute(block, 'rows', [(0, 1), (1, 0), (2, 3), (3, 2)])  8.2 us
    ppermute x1, waiting for transfers between devices, shards(): lax.ppermute(narrow, mesh_axes, spread(onward, outer_bands) + spread(firs...  5.68 us
    pallas_call x1, Pallas kernels, shards(): call(local_kernel, [((2, rows, *plane), BF16), ((2, rows + 2, *plane), F3...  4.23 us
    ppermute x1, starting transfers between devices, shards(): lax.ppermute(narrow, mesh_axes, spread(onward, outer_bands) + spread(firs...  3.92 us
    ppermute x1, starting transfers between devices, shards(): across = lax.ppermute(upper, 'rows', [(1, 2), (2, 1)])  3.9 us
    unnamed x10, local copies, waits for them, and re-layouts  3.81 us
    pallas_call x1, Pallas kernels, shards(): call(history_kernel, [((frames, rows, *plane), BF16), ((2, rows, *plane),...  3.44 us
    ppermute x1, starting transfers between devices, shards(): lax.ppermute(recent, mesh_axes, spread(straight, outer_bands + inner_band...  3.2 us
  transfers between devices with their start and end apart: 8, of which 3 were waited for; matrix products, arithmetic and copies ran while one was open for 0% of the time, Pallas kernels for 19%

profile of v5, /device:TPU:129, one launch (start us, length us, event | category | flops | bytes accessed | tf_op | source)
XLA Modules:
  0.0 44.5 jit_solution(17064594521812383253)
XLA Ops:
  0.0 0.0 copy-start
  0.0 1.1 %copy-done = bf16[4,8,96,128]{3,2,1,0:T(8,128)(2,1)S(1)} copy-done((bf16[4,8,96,128]{3,2,1,0:T(8,128)(2,1)S(1)}, bf16[4,8,96,128]{3,2,1,0:T(8,128)(2,1)}, u32[]{:S(2)}) %copy-start) | copy-done | bytes 786456
  1.1 0.0 copy-start.1
  1.1 0.3 shard_map.46
  1.5 3.2 %collective-permute-start.3 = (bf16[2,8,96,128]{3,2,1,0:T(8,128)(2,1)S(1)}, bf16[2,8,96,128]{3,2,1,0:T(8,128)(2,1)S(1)}, u32[]{:S(2)}, u32[]{:S(2)}) collective-permute-start(bf16[2,8,96,128]{3,2,1,0:T(8,128)(2,1)S(1)} %get-tuple-element.23), channel_id=1, source_target_pairs={{0,4},{3,7},{1,5},{2,6},{4,8},{7,11},{5,9},{6,10},{8,12},{11,15},{... | collective-permute-start | bytes 1179656 | tf_op jit(solution)/shard_map/ppermute | solution.py:311
  4.7 2.9 %collective-permute-start = (bf16[4,2,96,128]{3,2,1,0:T(8,128)(2,1)S(1)}, bf16[4,2,96,128]{3,2,1,0:T(8,128)(2,1)S(1)}, u32[]{:S(2)}, u32[]{:S(2)}) collective-permute-start(bf16[4,2,96,128]{3,2,1,0:T(8,128)(2,1)S(1)} %get-tuple-element.17), channel_id=1, source_target_pairs={{0,1},{1,0},{2,3},{3,2},{4,5},{5,4},{6,7},{7,6},{8,9},{9,8},{10,11... | collective-permute-start | bytes 589832 | tf_op jit(solution)/shard_map/ppermute | solution.py:285
  7.6 3.9 %collective-permute-start.1 = (bf16[4,2,96,128]{3,2,1,0:T(8,128)(2,1)S(1)}, bf16[4,2,96,128]{3,2,1,0:T(8,128)(2,1)S(1)}, u32[]{:S(2)}, u32[]{:S(2)}) collective-permute-start(bf16[4,2,96,128]{3,2,1,0:T(8,128)(2,1)S(1)} %get-tuple-element.18), channel_id=1, source_target_pairs={{1,2},{2,1},{5,6},{6,5},{9,10},{10,9},{13,14},{14,13},{17,18},{18,... | collective-permute-start | bytes 589832 | tf_op jit(solution)/shard_map/ppermute | solution.py:302
  11.5 0.0 copy-start.2
  11.5 1.3 %copy-done.2 = bf16[2,3,3,3,96,96]{5,4,3,2,1,0:T(8,128)(2,1)S(1)} copy-done((bf16[2,3,3,3,96,96]{5,4,3,2,1,0:T(8,128)(2,1)S(1)}, bf16[2,3,3,3,96,96]{5,4,3,2,1,0:T(8,128)(2,1)}, u32[]{:S(2)}) %copy-start.2) | copy-done | bytes 995352
  12.8 0.0 copy-start.3
  12.8 0.7 %copy-done.3 = f32[2,96]{1,0:T(2,128)S(1)} copy-done((f32[2,96]{1,0:T(2,128)S(1)}, f32[2,96]{1,0:T(2,128)}, u32[]{:S(2)}) %copy-start.3) | copy-done | bytes 792
  13.5 0.0 copy-start.4
  13.5 0.7 %copy-done.4 = f32[2,96]{1,0:T(2,128)S(1)} copy-done((f32[2,96]{1,0:T(2,128)S(1)}, f32[2,96]{1,0:T(2,128)}, u32[]{:S(2)}) %copy-start.4) | copy-done | bytes 792
  14.2 0.6 %shard_map.47 = (bf16[2,288,864]{2,1,0:T(8,128)(2,1)S(1)}, f32[2,96,128]{2,1,0:T(8,128)S(1)}, f32[2,96,128]{2,1,0:T(8,128)S(1)}) custom-call(bf16[2,3,864,96]{3,2,1,0:T(8,128)(2,1)S(1)} %bitcast.1, f32[2,96]{1,0:T(2,128)S(1)} %copy-done.3, f32[2,96]{1,0:T(2,128)S(1)} %copy-done.4), custom_call_target="tpu_custom_call" | custom-call | flops 1000000 | tf_op jit(solution)/shard_map/pallas_call | solution.py:320
  14.8 0.0 collective-permute-done.partner_ref
  14.8 0.3 collective-permute-done.1.across_ref
  15.1 0.0 copy-done.1
  15.1 4.2 %shard_map.48 = (bf16[2,8,96,128]{3,2,1,0:T(8,128)(2,1)S(1)}, f32[2,10,96,128]{3,2,1,0:T(8,128)S(1)}, f32[2,8,96,128]{3,2,1,0:T(8,128)S(1)}) custom-call(bf16[4,8,96,128]{3,2,1,0:T(8,128)(2,1)S(1)} %copy-done.1, bf16[4,2,96,128]{3,2,1,0:T(8,128)(2,1)S(1)} %collective-permute-done.partner_ref, bf16[4,2,96,128]{3,2,1,0:T(8,128)(2,1)S(1)} %collective-permute-done.1.across_ref, ...), custom_call_target="tpu_custom_call" | custom-call | tf_op jit(solution)/shard_map/pallas_call | solution.py:337
  19.3 2.9 %collective-permute-start.2 = (bf16[2,8,96,128]{3,2,1,0:T(8,128)(2,1)S(1)}, bf16[2,8,96,128]{3,2,1,0:T(8,128)(2,1)S(1)}, u32[]{:S(2)}, u32[]{:S(2)}) collective-permute-start(bf16[2,8,96,128]{3,2,1,0:T(8,128)(2,1)S(1)} %get-tuple-element.22), channel_id=1, source_target_pairs={{0,4},{4,8},{8,12},{12,16},{16,20},{20,24},{24,28},{28,32},{32,36}... | collective-permute-start | bytes 1179656 | tf_op jit(solution)/shard_map/ppermute | solution.py:351
  22.3 0.0 collective-permute-done.3.earlier_ref
  22.3 3.9 %collective-permute-start.4 = (bf16[2,4,96,128]{3,2,1,0:T(8,128)(2,1)S(1)}, bf16[2,4,96,128]{3,2,1,0:T(8,128)(2,1)S(1)}, u32[]{:S(2)}, u32[]{:S(2)}) collective-permute-start(bf16[2,4,96,128]{3,2,1,0:T(8,128)(2,1)S(1)} %shard_map.49), channel_id=1, source_target_pairs={{0,128},{3,131},{128,256},{131,259},{256,384},{259,387},{129,130},... | collective-permute-start | bytes 589832 | tf_op jit(solution)/shard_map/ppermute | solution.py:357
  26.3 0.7 %collective-permute-start.5 = (bf16[2,4,96,128]{3,2,1,0:T(8,128)(2,1)S(1)}, bf16[2,4,96,128]{3,2,1,0:T(8,128)(2,1)S(1)}, u32[]{:S(2)}, u32[]{:S(2)}) collective-permute-start(bf16[2,4,96,128]{3,2,1,0:T(8,128)(2,1)S(1)} %slice.8), channel_id=1, source_target_pairs={{0,128},{3,131},{128,256},{131,259},{256,384},{259,387}} | collective-permute-start | bytes 589832 | tf_op jit(solution)/shard_map/ppermute | solution.py:360
  27.0 1.3 %collective-permute-start.6 = (bf16[2,2,96,128]{3,2,1,0:T(8,128)(2,1)S(1)}, bf16[2,2,96,128]{3,2,1,0:T(8,128)(2,1)S(1)}, u32[]{:S(2)}, u32[]{:S(2)}) collective-permute-start(bf16[2,2,96,128]{3,2,1,0:T(8,128)(2,1)S(1)} %slice.9), channel_id=1, source_target_pairs={{1,5},{2,6},{5,9},{6,10},{9,13},{10,14},{13,17},{14,18},{17,21},{1... | collective-permute-start | bytes 294920 | tf_op jit(solution)/shard_map/ppermute | solution.py:353
  28.3 5.7 %collective-permute-done.4.narrow_ref = bf16[2,4,96,128]{3,2,1,0:T(8,128)(2,1)S(1)} collective-permute-done((bf16[2,4,96,128]{3,2,1,0:T(8,128)(2,1)S(1)}, bf16[2,4,96,128]{3,2,1,0:T(8,128)(2,1)S(1)}, u32[]{:S(2)}, u32[]{:S(2)}) %collective-permute-start.4) | collective-permute-done | bytes 196640 | tf_op jit(solution)/shard_map/ppermute | solution.py:357
  33.9 0.0 collective-permute-done.5.rest_ref
  34.0 5.3 %collective-permute-start.7 = (bf16[2,2,96,128]{3,2,1,0:T(8,128)(2,1)S(1)}, bf16[2,2,96,128]{3,2,1,0:T(8,128)(2,1)S(1)}, u32[]{:S(2)}, u32[]{:S(2)}) collective-permute-start(bf16[2,2,96,128]{3,2,1,0:T(8,128)(2,1)S(1)} %shard_map.50), channel_id=1, source_target_pairs={{0,1},{1,0},{2,3},{3,2},{4,5},{5,4},{6,7},{7,6},{8,9},{9,8},{10,11... | collective-permute-start | bytes 294920 | tf_op jit(solution)/shard_map/ppermute | solution.py:285
  39.3 0.0 collective-permute-done.6.corner_ref
  39.3 0.9 %collective-permute-done.7.partner_ref = bf16[2,2,96,128]{3,2,1,0:T(8,128)(2,1)S(1)} collective-permute-done((bf16[2,2,96,128]{3,2,1,0:T(8,128)(2,1)S(1)}, bf16[2,2,96,128]{3,2,1,0:T(8,128)(2,1)S(1)}, u32[]{:S(2)}, u32[]{:S(2)}) %collective-permute-start.7) | collective-permute-done | bytes 98336 | tf_op jit(solution)/shard_map/ppermute | solution.py:285
  40.3 3.4 %shard_map.51 = (bf16[4,8,96,128]{3,2,1,0:T(8,128)(2,1)}, f32[2,8,96,128]{3,2,1,0:T(8,128)S(1)}) custom-call(bf16[2,8,96,128]{3,2,1,0:T(8,128)(2,1)S(1)} %collective-permute-done.3.earlier_ref, bf16[2,4,96,128]{3,2,1,0:T(8,128)(2,1)S(1)} %collective-permute-done.4.narrow_ref, bf16[2,4,96,128]{3,2,1,0:T(8,128)(2,1)S(1)} %collective-permute-done.5.rest_ref, ...), custom_call_target="tpu_custom_call" | custom-call | tf_op jit(solution)/shard_map/pallas_call | solution.py:363
  43.7 0.0 collective-permute-done.2.partial_ref
  43.7 0.8 %shard_map.52 = bf16[4,8,96,128]{3,2,1,0:T(8,128)(2,1)} custom-call(bf16[2,8,96,128]{3,2,1,0:T(8,128)(2,1)S(1)} %collective-permute-done.2.partial_ref, f32[2,8,96,128]{3,2,1,0:T(8,128)S(1)} %get-tuple-element.27.first_ref, bf16[4,8,96,128]{3,2,1,0:T(8,128)(2,1)} %get-tuple-element.28._), custom_call_target="tpu_custom_call", output_to_operand_aliasing={{}: (2, {})} | custom-call | flops 1000000 | bytes 2000000 | tf_op jit(solution)/shard_map/pallas_call | solution.py:374
  (4 shorter events, 0.1 us)
Async XLA Ops:
  0.0 1.1 %copy-start = (bf16[4,8,96,128]{3,2,1,0:T(8,128)(2,1)S(1)}, bf16[4,8,96,128]{3,2,1,0:T(8,128)(2,1)}, u32[]{:S(2)}) copy-start(bf16[4,8,96,128]{3,2,1,0:T(8,128)(2,1)} %stream_ref.5) | copy-start | bytes 2359300
  1.1 14.0 %copy-start.1 = (bf16[4,8,96,128]{3,2,1,0:T(8,128)(2,1)S(1)}, bf16[4,8,96,128]{3,2,1,0:T(8,128)(2,1)}, u32[]{:S(2)}) copy-start(bf16[4,8,96,128]{3,2,1,0:T(8,128)(2,1)} %stream_ref.5) | copy-start | bytes 2359300
  1.5 20.8 %collective-permute-start.3 = (bf16[2,8,96,128]{3,2,1,0:T(8,128)(2,1)S(1)}, bf16[2,8,96,128]{3,2,1,0:T(8,128)(2,1)S(1)}, u32[]{:S(2)}, u32[]{:S(2)}) collective-permute-start(bf16[2,8,96,128]{3,2,1,0:T(8,128)(2,1)S(1)} %get-tuple-element.23), channel_id=1, source_target_pairs={{0,4},{3,7},{1,5},{2,6},{4,8},{7,11},{5,9},{6,10},{8,12},{11,15},{... | collective-permute-start | bytes 1179656 | tf_op jit(solution)/shard_map/ppermute | solution.py:311
  4.7 10.1 %collective-permute-start = (bf16[4,2,96,128]{3,2,1,0:T(8,128)(2,1)S(1)}, bf16[4,2,96,128]{3,2,1,0:T(8,128)(2,1)S(1)}, u32[]{:S(2)}, u32[]{:S(2)}) collective-permute-start(bf16[4,2,96,128]{3,2,1,0:T(8,128)(2,1)S(1)} %get-tuple-element.17), channel_id=1, source_target_pairs={{0,1},{1,0},{2,3},{3,2},{4,5},{5,4},{6,7},{7,6},{8,9},{9,8},{10,11... | collective-permute-start | bytes 589832 | tf_op jit(solution)/shard_map/ppermute | solution.py:285
  7.6 7.5 %collective-permute-start.1 = (bf16[4,2,96,128]{3,2,1,0:T(8,128)(2,1)S(1)}, bf16[4,2,96,128]{3,2,1,0:T(8,128)(2,1)S(1)}, u32[]{:S(2)}, u32[]{:S(2)}) collective-permute-start(bf16[4,2,96,128]{3,2,1,0:T(8,128)(2,1)S(1)} %get-tuple-element.18), channel_id=1, source_target_pairs={{1,2},{2,1},{5,6},{6,5},{9,10},{10,9},{13,14},{14,13},{17,18},{18,... | collective-permute-start | bytes 589832 | tf_op jit(solution)/shard_map/ppermute | solution.py:302
  11.5 1.3 %copy-start.2 = (bf16[2,3,3,3,96,96]{5,4,3,2,1,0:T(8,128)(2,1)S(1)}, bf16[2,3,3,3,96,96]{5,4,3,2,1,0:T(8,128)(2,1)}, u32[]{:S(2)}) copy-start(bf16[2,3,3,3,96,96]{5,4,3,2,1,0:T(8,128)(2,1)} %param.6) | copy-start | bytes 2985988
  12.8 0.7 %copy-start.3 = (f32[2,96]{1,0:T(2,128)S(1)}, f32[2,96]{1,0:T(2,128)}, u32[]{:S(2)}) copy-start(f32[2,96]{1,0:T(2,128)} %all_gains_ref.1) | copy-start | bytes 2308
  13.5 0.7 %copy-start.4 = (f32[2,96]{1,0:T(2,128)S(1)}, f32[2,96]{1,0:T(2,128)}, u32[]{:S(2)}) copy-start(f32[2,96]{1,0:T(2,128)} %all_biases_ref.1) | copy-start | bytes 2308
  19.3 24.4 %collective-permute-start.2 = (bf16[2,8,96,128]{3,2,1,0:T(8,128)(2,1)S(1)}, bf16[2,8,96,128]{3,2,1,0:T(8,128)(2,1)S(1)}, u32[]{:S(2)}, u32[]{:S(2)}) collective-permute-start(bf16[2,8,96,128]{3,2,1,0:T(8,128)(2,1)S(1)} %get-tuple-element.22), channel_id=1, source_target_pairs={{0,4},{4,8},{8,12},{12,16},{16,20},{20,24},{24,28},{28,32},{32,36}... | collective-permute-start | bytes 1179656 | tf_op jit(solution)/shard_map/ppermute | solution.py:351
  22.3 11.6 %collective-permute-start.4 = (bf16[2,4,96,128]{3,2,1,0:T(8,128)(2,1)S(1)}, bf16[2,4,96,128]{3,2,1,0:T(8,128)(2,1)S(1)}, u32[]{:S(2)}, u32[]{:S(2)}) collective-permute-start(bf16[2,4,96,128]{3,2,1,0:T(8,128)(2,1)S(1)} %shard_map.49), channel_id=1, source_target_pairs={{0,128},{3,131},{128,256},{131,259},{256,384},{259,387},{129,130},... | collective-permute-start | bytes 589832 | tf_op jit(solution)/shard_map/ppermute | solution.py:357
  26.3 7.7 %collective-permute-start.5 = (bf16[2,4,96,128]{3,2,1,0:T(8,128)(2,1)S(1)}, bf16[2,4,96,128]{3,2,1,0:T(8,128)(2,1)S(1)}, u32[]{:S(2)}, u32[]{:S(2)}) collective-permute-start(bf16[2,4,96,128]{3,2,1,0:T(8,128)(2,1)S(1)} %slice.8), channel_id=1, source_target_pairs={{0,128},{3,131},{128,256},{131,259},{256,384},{259,387}} | collective-permute-start | bytes 589832 | tf_op jit(solution)/shard_map/ppermute | solution.py:360
  27.0 12.4 %collective-permute-start.6 = (bf16[2,2,96,128]{3,2,1,0:T(8,128)(2,1)S(1)}, bf16[2,2,96,128]{3,2,1,0:T(8,128)(2,1)S(1)}, u32[]{:S(2)}, u32[]{:S(2)}) collective-permute-start(bf16[2,2,96,128]{3,2,1,0:T(8,128)(2,1)S(1)} %slice.9), channel_id=1, source_target_pairs={{1,5},{2,6},{5,9},{6,10},{9,13},{10,14},{13,17},{14,18},{17,21},{1... | collective-permute-start | bytes 294920 | tf_op jit(solution)/shard_map/ppermute | solution.py:353
  34.0 6.3 %collective-permute-start.7 = (bf16[2,2,96,128]{3,2,1,0:T(8,128)(2,1)S(1)}, bf16[2,2,96,128]{3,2,1,0:T(8,128)(2,1)S(1)}, u32[]{:S(2)}, u32[]{:S(2)}) collective-permute-start(bf16[2,2,96,128]{3,2,1,0:T(8,128)(2,1)S(1)} %shard_map.50), channel_id=1, source_target_pairs={{0,1},{1,0},{2,3},{3,2},{4,5},{5,4},{6,7},{7,6},{8,9},{9,8},{10,11... | collective-permute-start | bytes 294920 | tf_op jit(solution)/shard_map/ppermute | solution.py:285

commit v6 on v5

--- a/solution.py
+++ b/solution.py
@@ -118,7 +118,7 @@
 
 def narrow_kernel(earlier_ref, out_ref):
     half = out_ref.shape[1]
-    start = jnp.where(lax.axis_index("rows") == 1, half, 0)
+    start = jnp.where(lax.axis_index("rows") == 1, earlier_ref.shape[1] - half, 0)
     out_ref[...] = earlier_ref[:, pl.ds(start, half)]
 
 
@@ -127,7 +127,7 @@
     rows = earlier_ref.shape[1]
     odd = lax.axis_index("rows") % 2 == 1
     near = pl.ds(jnp.where(odd, 0, rows - 2), 2)
-    relayed = jnp.where(odd, narrow_ref[:, :2], rest_ref[:, rows // 2 - 2 :])
+    relayed = jnp.where(odd, narrow_ref[:, :2], rest_ref[:, rest_ref.shape[1] - 2 :])
     out_ref[...] = jnp.where(relay, relayed, earlier_ref[:, near])
 
 
@@ -206,12 +206,12 @@
     relay, swap = first_block_bands()
 
     def own(frame, row):
-        half = rows // 2
+        half = narrow_ref.shape[1]
         relayed = narrow_ref[frame, row] if row < half else rest_ref[frame, row - half]
         return jnp.where(relay, relayed, earlier_ref[frame, row])
 
     def across(frame, row, start):
-        swapped = narrow_ref[frame, row + (rows // 2 - 2 if start == 0 else 0)]
+        swapped = narrow_ref[frame, row + (narrow_ref.shape[1] - 2 if start == 0 else 0)]
         return jnp.where(swap, swapped, corner_ref[frame, row])
 
     activate_rows(
@@ -352,7 +352,7 @@
     corner, sent = lax.optimization_barrier((across[frames - 2 :], sent))
     corner = lax.ppermute(corner, mesh_axes, spread(straight, inner_bands))
     earlier, sent = lax.optimization_barrier((earlier, sent))
-    half = rows // 2
+    half = rows // 2 - 1
     (narrow,) = call(narrow_kernel, [((2, half, *plane), BF16)])(earlier)
     narrow = lax.ppermute(
         narrow, mesh_axes, spread(onward, outer_bands) + spread(first_blocks, [(1, 2), (2, 1)])

time: 44.9 us -> 44.9 us (level)
  no operation moved by 1% of the time
where the time goes in v6:
time: 44.9 us; the launch traced here: 44.5 us
  starting transfers between devices  23.9 us (53%)
  Pallas kernels  9.5 us (21%)
  waiting for transfers between devices  7.15 us (16%)
  local copies, waits for them, and re-layouts  3.84 us (9%)
    ppermute x2, starting transfers between devices, partners(): return lax.ppermute(block, 'rows', [(0, 1), (1, 0), (2, 3), (3, 2)])  7.95 us
    ppermute x1, waiting for transfers between devices, shards(): lax.ppermute(narrow, mesh_axes, spread(onward, outer_bands) + spread(firs...  5.91 us
    pallas_call x1, Pallas kernels, shards(): call(local_kernel, [((2, rows, *plane), BF16), ((2, rows + 2, *plane), F3...  4.23 us
    ppermute x1, starting transfers between devices, shards(): lax.ppermute(narrow, mesh_axes, spread(onward, outer_bands) + spread(firs...  3.92 us
    ppermute x1, starting transfers between devices, shards(): across = lax.ppermute(upper, 'rows', [(1, 2), (2, 1)])  3.9 us
    unnamed x10, local copies, waits for them, and re-layouts  3.81 us
    pallas_call x1, Pallas kernels, shards(): call(history_kernel, [((frames, rows, *plane), BF16), ((2, rows, *plane),...  3.44 us
    ppermute x1, starting transfers between devices, shards(): lax.ppermute(recent, mesh_axes, spread(straight, outer_bands + inner_band...  3.2 us
  transfers between devices with their start and end apart: 8, of which 3 were waited for; matrix products, arithmetic and copies ran while one was open for 0% of the time, Pallas kernels for 19%

profile of v6, /device:TPU:129, one launch (start us, length us, event | category | flops | bytes accessed | tf_op | source)
XLA Modules:
  0.0 44.5 jit_solution(10455338468622195922)
XLA Ops:
  0.0 0.0 copy-start
  0.0 1.1 %copy-done = bf16[4,8,96,128]{3,2,1,0:T(8,128)(2,1)S(1)} copy-done((bf16[4,8,96,128]{3,2,1,0:T(8,128)(2,1)S(1)}, bf16[4,8,96,128]{3,2,1,0:T(8,128)(2,1)}, u32[]{:S(2)}) %copy-start) | copy-done | bytes 786456
  1.1 0.0 copy-start.1
  1.1 0.3 shard_map.46
  1.5 3.2 %collective-permute-start.3 = (bf16[2,8,96,128]{3,2,1,0:T(8,128)(2,1)S(1)}, bf16[2,8,96,128]{3,2,1,0:T(8,128)(2,1)S(1)}, u32[]{:S(2)}, u32[]{:S(2)}) collective-permute-start(bf16[2,8,96,128]{3,2,1,0:T(8,128)(2,1)S(1)} %get-tuple-element.23), channel_id=1, source_target_pairs={{0,4},{3,7},{1,5},{2,6},{4,8},{7,11},{5,9},{6,10},{8,12},{11,15},{... | collective-permute-start | bytes 1179656 | tf_op jit(solution)/shard_map/ppermute | solution.py:311
  4.7 2.9 %collective-permute-start = (bf16[4,2,96,128]{3,2,1,0:T(8,128)(2,1)S(1)}, bf16[4,2,96,128]{3,2,1,0:T(8,128)(2,1)S(1)}, u32[]{:S(2)}, u32[]{:S(2)}) collective-permute-start(bf16[4,2,96,128]{3,2,1,0:T(8,128)(2,1)S(1)} %get-tuple-element.17), channel_id=1, source_target_pairs={{0,1},{1,0},{2,3},{3,2},{4,5},{5,4},{6,7},{7,6},{8,9},{9,8},{10,11... | collective-permute-start | bytes 589832 | tf_op jit(solution)/shard_map/ppermute | solution.py:285
  7.6 3.9 %collective-permute-start.1 = (bf16[4,2,96,128]{3,2,1,0:T(8,128)(2,1)S(1)}, bf16[4,2,96,128]{3,2,1,0:T(8,128)(2,1)S(1)}, u32[]{:S(2)}, u32[]{:S(2)}) collective-permute-start(bf16[4,2,96,128]{3,2,1,0:T(8,128)(2,1)S(1)} %get-tuple-element.18), channel_id=1, source_target_pairs={{1,2},{2,1},{5,6},{6,5},{9,10},{10,9},{13,14},{14,13},{17,18},{18,... | collective-permute-start | bytes 589832 | tf_op jit(solution)/shard_map/ppermute | solution.py:302
  11.5 0.0 copy-start.2
  11.5 1.3 %copy-done.2 = bf16[2,3,3,3,96,96]{5,4,3,2,1,0:T(8,128)(2,1)S(1)} copy-done((bf16[2,3,3,3,96,96]{5,4,3,2,1,0:T(8,128)(2,1)S(1)}, bf16[2,3,3,3,96,96]{5,4,3,2,1,0:T(8,128)(2,1)}, u32[]{:S(2)}) %copy-start.2) | copy-done | bytes 995352
  12.8 0.0 copy-start.3
  12.8 0.7 %copy-done.3 = f32[2,96]{1,0:T(2,128)S(1)} copy-done((f32[2,96]{1,0:T(2,128)S(1)}, f32[2,96]{1,0:T(2,128)}, u32[]{:S(2)}) %copy-start.3) | copy-done | bytes 792
  13.5 0.0 copy-start.4
  13.5 0.7 %copy-done.4 = f32[2,96]{1,0:T(2,128)S(1)} copy-done((f32[2,96]{1,0:T(2,128)S(1)}, f32[2,96]{1,0:T(2,128)}, u32[]{:S(2)}) %copy-start.4) | copy-done | bytes 792
  14.2 0.6 %shard_map.47 = (bf16[2,288,864]{2,1,0:T(8,128)(2,1)S(1)}, f32[2,96,128]{2,1,0:T(8,128)S(1)}, f32[2,96,128]{2,1,0:T(8,128)S(1)}) custom-call(bf16[2,3,864,96]{3,2,1,0:T(8,128)(2,1)S(1)} %bitcast.1, f32[2,96]{1,0:T(2,128)S(1)} %copy-done.3, f32[2,96]{1,0:T(2,128)S(1)} %copy-done.4), custom_call_target="tpu_custom_call" | custom-call | flops 1000000 | tf_op jit(solution)/shard_map/pallas_call | solution.py:320
  14.8 0.0 collective-permute-done.partner_ref
  14.8 0.3 collective-permute-done.1.across_ref
  15.1 0.0 copy-done.1
  15.1 4.2 %shard_map.48 = (bf16[2,8,96,128]{3,2,1,0:T(8,128)(2,1)S(1)}, f32[2,10,96,128]{3,2,1,0:T(8,128)S(1)}, f32[2,8,96,128]{3,2,1,0:T(8,128)S(1)}) custom-call(bf16[4,8,96,128]{3,2,1,0:T(8,128)(2,1)S(1)} %copy-done.1, bf16[4,2,96,128]{3,2,1,0:T(8,128)(2,1)S(1)} %collective-permute-done.partner_ref, bf16[4,2,96,128]{3,2,1,0:T(8,128)(2,1)S(1)} %collective-permute-done.1.across_ref, ...), custom_call_target="tpu_custom_call" | custom-call | tf_op jit(solution)/shard_map/pallas_call | solution.py:337
  19.3 2.9 %collective-permute-start.2 = (bf16[2,8,96,128]{3,2,1,0:T(8,128)(2,1)S(1)}, bf16[2,8,96,128]{3,2,1,0:T(8,128)(2,1)S(1)}, u32[]{:S(2)}, u32[]{:S(2)}) collective-permute-start(bf16[2,8,96,128]{3,2,1,0:T(8,128)(2,1)S(1)} %get-tuple-element.22), channel_id=1, source_target_pairs={{0,4},{4,8},{8,12},{12,16},{16,20},{20,24},{24,28},{28,32},{32,36}... | collective-permute-start | bytes 1179656 | tf_op jit(solution)/shard_map/ppermute | solution.py:351
  22.3 0.0 collective-permute-done.3.earlier_ref
  22.3 0.7 %collective-permute-start.5 = (bf16[2,5,96,128]{3,2,1,0:T(8,128)(2,1)S(1)}, bf16[2,5,96,128]{3,2,1,0:T(8,128)(2,1)S(1)}, u32[]{:S(2)}, u32[]{:S(2)}) collective-permute-start(bf16[2,5,96,128]{3,2,1,0:T(8,128)(2,1)S(1)} %slice.8), channel_id=1, source_target_pairs={{0,128},{3,131},{128,256},{131,259},{256,384},{259,387}} | collective-permute-start | bytes 737288 | tf_op jit(solution)/shard_map/ppermute | solution.py:360
  23.0 3.9 %collective-permute-start.4 = (bf16[2,3,96,128]{3,2,1,0:T(8,128)(2,1)S(1)}, bf16[2,3,96,128]{3,2,1,0:T(8,128)(2,1)S(1)}, u32[]{:S(2)}, u32[]{:S(2)}) collective-permute-start(bf16[2,3,96,128]{3,2,1,0:T(8,128)(2,1)S(1)} %shard_map.49), channel_id=1, source_target_pairs={{0,128},{3,131},{128,256},{131,259},{256,384},{259,387},{129,130},... | collective-permute-start | bytes 442376 | tf_op jit(solution)/shard_map/ppermute | solution.py:357
  27.0 1.3 %collective-permute-start.6 = (bf16[2,2,96,128]{3,2,1,0:T(8,128)(2,1)S(1)}, bf16[2,2,96,128]{3,2,1,0:T(8,128)(2,1)S(1)}, u32[]{:S(2)}, u32[]{:S(2)}) collective-permute-start(bf16[2,2,96,128]{3,2,1,0:T(8,128)(2,1)S(1)} %slice.9), channel_id=1, source_target_pairs={{1,5},{2,6},{5,9},{6,10},{9,13},{10,14},{13,17},{14,18},{17,21},{1... | collective-permute-start | bytes 294920 | tf_op jit(solution)/shard_map/ppermute | solution.py:353
  28.3 5.9 %collective-permute-done.4.narrow_ref = bf16[2,3,96,128]{3,2,1,0:T(8,128)(2,1)S(1)} collective-permute-done((bf16[2,3,96,128]{3,2,1,0:T(8,128)(2,1)S(1)}, bf16[2,3,96,128]{3,2,1,0:T(8,128)(2,1)S(1)}, u32[]{:S(2)}, u32[]{:S(2)}) %collective-permute-start.4) | collective-permute-done | bytes 147488 | tf_op jit(solution)/shard_map/ppermute | solution.py:357
  34.2 0.0 collective-permute-done.5.rest_ref
  34.2 5.1 %collective-permute-start.7 = (bf16[2,2,96,128]{3,2,1,0:T(8,128)(2,1)S(1)}, bf16[2,2,96,128]{3,2,1,0:T(8,128)(2,1)S(1)}, u32[]{:S(2)}, u32[]{:S(2)}) collective-permute-start(bf16[2,2,96,128]{3,2,1,0:T(8,128)(2,1)S(1)} %shard_map.50), channel_id=1, source_target_pairs={{0,1},{1,0},{2,3},{3,2},{4,5},{5,4},{6,7},{7,6},{8,9},{9,8},{10,11... | collective-permute-start | bytes 294920 | tf_op jit(solution)/shard_map/ppermute | solution.py:285
  39.3 0.0 collective-permute-done.6.corner_ref
  39.3 0.9 %collective-permute-done.7.partner_ref = bf16[2,2,96,128]{3,2,1,0:T(8,128)(2,1)S(1)} collective-permute-done((bf16[2,2,96,128]{3,2,1,0:T(8,128)(2,1)S(1)}, bf16[2,2,96,128]{3,2,1,0:T(8,128)(2,1)S(1)}, u32[]{:S(2)}, u32[]{:S(2)}) %collective-permute-start.7) | collective-permute-done | bytes 98336 | tf_op jit(solution)/shard_map/ppermute | solution.py:285
  40.2 3.4 %shard_map.51 = (bf16[4,8,96,128]{3,2,1,0:T(8,128)(2,1)}, f32[2,8,96,128]{3,2,1,0:T(8,128)S(1)}) custom-call(bf16[2,8,96,128]{3,2,1,0:T(8,128)(2,1)S(1)} %collective-permute-done.3.earlier_ref, bf16[2,3,96,128]{3,2,1,0:T(8,128)(2,1)S(1)} %collective-permute-done.4.narrow_ref, bf16[2,5,96,128]{3,2,1,0:T(8,128)(2,1)S(1)} %collective-permute-done.5.rest_ref, ...), custom_call_target="tpu_custom_call" | custom-call | tf_op jit(solution)/shard_map/pallas_call | solution.py:363
  43.7 0.0 collective-permute-done.2.partial_ref
  43.7 0.8 %shard_map.52 = bf16[4,8,96,128]{3,2,1,0:T(8,128)(2,1)} custom-call(bf16[2,8,96,128]{3,2,1,0:T(8,128)(2,1)S(1)} %collective-permute-done.2.partial_ref, f32[2,8,96,128]{3,2,1,0:T(8,128)S(1)} %get-tuple-element.27.first_ref, bf16[4,8,96,128]{3,2,1,0:T(8,128)(2,1)} %get-tuple-element.28._), custom_call_target="tpu_custom_call", output_to_operand_aliasing={{}: (2, {})} | custom-call | flops 1000000 | bytes 2000000 | tf_op jit(solution)/shard_map/pallas_call | solution.py:374
  (4 shorter events, 0.1 us)
Async XLA Ops:
  0.0 1.1 %copy-start = (bf16[4,8,96,128]{3,2,1,0:T(8,128)(2,1)S(1)}, bf16[4,8,96,128]{3,2,1,0:T(8,128)(2,1)}, u32[]{:S(2)}) copy-start(bf16[4,8,96,128]{3,2,1,0:T(8,128)(2,1)} %stream_ref.5) | copy-start | bytes 2359300
  1.1 14.0 %copy-start.1 = (bf16[4,8,96,128]{3,2,1,0:T(8,128)(2,1)S(1)}, bf16[4,8,96,128]{3,2,1,0:T(8,128)(2,1)}, u32[]{:S(2)}) copy-start(bf16[4,8,96,128]{3,2,1,0:T(8,128)(2,1)} %stream_ref.5) | copy-start | bytes 2359300
  1.5 20.8 %collective-permute-start.3 = (bf16[2,8,96,128]{3,2,1,0:T(8,128)(2,1)S(1)}, bf16[2,8,96,128]{3,2,1,0:T(8,128)(2,1)S(1)}, u32[]{:S(2)}, u32[]{:S(2)}) collective-permute-start(bf16[2,8,96,128]{3,2,1,0:T(8,128)(2,1)S(1)} %get-tuple-element.23), channel_id=1, source_target_pairs={{0,4},{3,7},{1,5},{2,6},{4,8},{7,11},{5,9},{6,10},{8,12},{11,15},{... | collective-permute-start | bytes 1179656 | tf_op jit(solution)/shard_map/ppermute | solution.py:311
  4.7 10.1 %collective-permute-start = (bf16[4,2,96,128]{3,2,1,0:T(8,128)(2,1)S(1)}, bf16[4,2,96,128]{3,2,1,0:T(8,128)(2,1)S(1)}, u32[]{:S(2)}, u32[]{:S(2)}) collective-permute-start(bf16[4,2,96,128]{3,2,1,0:T(8,128)(2,1)S(1)} %get-tuple-element.17), channel_id=1, source_target_pairs={{0,1},{1,0},{2,3},{3,2},{4,5},{5,4},{6,7},{7,6},{8,9},{9,8},{10,11... | collective-permute-start | bytes 589832 | tf_op jit(solution)/shard_map/ppermute | solution.py:285
  7.6 7.5 %collective-permute-start.1 = (bf16[4,2,96,128]{3,2,1,0:T(8,128)(2,1)S(1)}, bf16[4,2,96,128]{3,2,1,0:T(8,128)(2,1)S(1)}, u32[]{:S(2)}, u32[]{:S(2)}) collective-permute-start(bf16[4,2,96,128]{3,2,1,0:T(8,128)(2,1)S(1)} %get-tuple-element.18), channel_id=1, source_target_pairs={{1,2},{2,1},{5,6},{6,5},{9,10},{10,9},{13,14},{14,13},{17,18},{18,... | collective-permute-start | bytes 589832 | tf_op jit(solution)/shard_map/ppermute | solution.py:302
  11.5 1.3 %copy-start.2 = (bf16[2,3,3,3,96,96]{5,4,3,2,1,0:T(8,128)(2,1)S(1)}, bf16[2,3,3,3,96,96]{5,4,3,2,1,0:T(8,128)(2,1)}, u32[]{:S(2)}) copy-start(bf16[2,3,3,3,96,96]{5,4,3,2,1,0:T(8,128)(2,1)} %param.6) | copy-start | bytes 2985988
  12.8 0.7 %copy-start.3 = (f32[2,96]{1,0:T(2,128)S(1)}, f32[2,96]{1,0:T(2,128)}, u32[]{:S(2)}) copy-start(f32[2,96]{1,0:T(2,128)} %all_gains_ref.1) | copy-start | bytes 2308
  13.5 0.7 %copy-start.4 = (f32[2,96]{1,0:T(2,128)S(1)}, f32[2,96]{1,0:T(2,128)}, u32[]{:S(2)}) copy-start(f32[2,96]{1,0:T(2,128)} %all_biases_ref.1) | copy-start | bytes 2308
  19.3 24.3 %collective-permute-start.2 = (bf16[2,8,96,128]{3,2,1,0:T(8,128)(2,1)S(1)}, bf16[2,8,96,128]{3,2,1,0:T(8,128)(2,1)S(1)}, u32[]{:S(2)}, u32[]{:S(2)}) collective-permute-start(bf16[2,8,96,128]{3,2,1,0:T(8,128)(2,1)S(1)} %get-tuple-element.22), channel_id=1, source_target_pairs={{0,4},{4,8},{8,12},{12,16},{16,20},{20,24},{24,28},{28,32},{32,36}... | collective-permute-start | bytes 1179656 | tf_op jit(solution)/shard_map/ppermute | solution.py:351
  22.3 11.9 %collective-permute-start.5 = (bf16[2,5,96,128]{3,2,1,0:T(8,128)(2,1)S(1)}, bf16[2,5,96,128]{3,2,1,0:T(8,128)(2,1)S(1)}, u32[]{:S(2)}, u32[]{:S(2)}) collective-permute-start(bf16[2,5,96,128]{3,2,1,0:T(8,128)(2,1)S(1)} %slice.8), channel_id=1, source_target_pairs={{0,128},{3,131},{128,256},{131,259},{256,384},{259,387}} | collective-permute-start | bytes 737288 | tf_op jit(solution)/shard_map/ppermute | solution.py:360
  23.0 11.2 %collective-permute-start.4 = (bf16[2,3,96,128]{3,2,1,0:T(8,128)(2,1)S(1)}, bf16[2,3,96,128]{3,2,1,0:T(8,128)(2,1)S(1)}, u32[]{:S(2)}, u32[]{:S(2)}) collective-permute-start(bf16[2,3,96,128]{3,2,1,0:T(8,128)(2,1)S(1)} %shard_map.49), channel_id=1, source_target_pairs={{0,128},{3,131},{128,256},{131,259},{256,384},{259,387},{129,130},... | collective-permute-start | bytes 442376 | tf_op jit(solution)/shard_map/ppermute | solution.py:357
  27.0 12.4 %collective-permute-start.6 = (bf16[2,2,96,128]{3,2,1,0:T(8,128)(2,1)S(1)}, bf16[2,2,96,128]{3,2,1,0:T(8,128)(2,1)S(1)}, u32[]{:S(2)}, u32[]{:S(2)}) collective-permute-start(bf16[2,2,96,128]{3,2,1,0:T(8,128)(2,1)S(1)} %slice.9), channel_id=1, source_target_pairs={{1,5},{2,6},{5,9},{6,10},{9,13},{10,14},{13,17},{14,18},{17,21},{1... | collective-permute-start | bytes 294920 | tf_op jit(solution)/shard_map/ppermute | solution.py:353
  34.2 6.0 %collective-permute-start.7 = (bf16[2,2,96,128]{3,2,1,0:T(8,128)(2,1)S(1)}, bf16[2,2,96,128]{3,2,1,0:T(8,128)(2,1)S(1)}, u32[]{:S(2)}, u32[]{:S(2)}) collective-permute-start(bf16[2,2,96,128]{3,2,1,0:T(8,128)(2,1)S(1)} %shard_map.50), channel_id=1, source_target_pairs={{0,1},{1,0},{2,3},{3,2},{4,5},{5,4},{6,7},{7,6},{8,9},{9,8},{10,11... | collective-permute-start | bytes 294920 | tf_op jit(solution)/shard_map/ppermute | solution.py:285
